TPU v7x, 512 devices: a whole 4x8x8 slice. The times are simulated.
512 devices in a mesh: slab: 8 (over y), rve: 64 (over x, z, core).
Axes of the slice: x: 4, y: 8, z: 8, core: 2. Of those that a mesh axis runs over, the one named last changes fastest.
Arguments:
- macro_field: float32 [3, 65536], P(None, ('slab', 'rve')), may hold values from -6 to 6
- rve_owner: int32 [65536, 1], P(('slab', 'rve')), may hold values from 0 to 63; in each aligned block of 128 rows (0 to 127, 128 to 255, ...) at most 4 rows name the same one
- potential: float32 [65536, 512], P(('slab', 'rve')), may hold values from -3 to 3
- switch_words: int32 [131072, 512], P(('slab', 'rve')), may hold values from 0 to 15
- permeability: float32 [131072, 512], P(('slab', 'rve')), may hold values from 0.5 to 4
- coercivity: float32 [131072, 512], P(('slab', 'rve')), may hold values from 0.5 to 2
- grain_axes: float32 [3, 131072, 512], P(None, ('slab', 'rve')), may hold values from 0.5 to 2
- hyst_axis: float32 [3, 4], replicated, may hold values from 0.05 to 1
- hyst_low: float32 [4], replicated, may hold values from -1.5 to -0.1
- hyst_high: float32 [4], replicated, may hold values from 0.1 to 1.5
- hyst_weight: float32 [4], replicated, may hold values from 0.2 to 1
- grad_weights: float32 [3, 8, 65536], P(None, None, ('slab', 'rve')), may hold values from -0.3 to 0.3
- connectivity: int32 [8, 65536], P(None, ('slab', 'rve')), may hold values from 0 to 44, as said below
- node_order: int32 [23040], P(('slab', 'rve')), may hold values from 0 to 44, as said below
Outputs:
- potential_new: float32 [65536, 512], P(('slab', 'rve'))
- tangent: float32 [3, 3, 65536], P(None, None, ('slab', 'rve'))
- residual: float32 [23040], P(('slab', 'rve'))
Inputs may be any that keep to these rules, and one draw needn't show every extreme that they name: `rve_owner`: owner of a point's RVE along rve, in the point's slab. Among the 128 points of one block at most 4 name the same owner, a bound that some block reaches. `switch_words`: bit k (k below 4) of a voxel's word is hysteron k's last switching state, 1 for up. `connectivity`: A block holds 2 x 2 x 4 hexahedra of 8 points each; the corners of a point's hexahedron, corner a at offsets (a // 4, a // 2 % 2, a % 2), as local node numbers agreeing with node_order. `node_order`: for each block a permutation of the local node numbers, listed by structured position with z fastest.
All inputs are finite; a program needn't handle non-finite values.
Results may differ from a plain program's by a relative error of at most 0.0003.
Values sent between devices are 32-bit elements; how exact they have to be, the bound alone decides.
A program may use at most 64 MiB of HBM per device.

v0:
```python
import jax
import jax.numpy as jnp
from jax import lax
from jax.sharding import PartitionSpec as P

RES = 8
NHYS = 4
SWEEPS = 2
EX = 2
EY = 2
EZ = 4


slope_gain = 2.0
diag_boost = 1.5
highest = lax.Precision.HIGHEST


def extended(block, sides, width):
    for axis, dim in sides:
        count = lax.axis_size(axis)
        forward = [(i, i + 1) for i in range(count - 1)]
        backward = [(target, source) for source, target in forward]
        low = lax.ppermute(
            lax.slice_in_dim(block, block.shape[dim] - width, None, axis=dim), axis, forward
        )
        high = lax.ppermute(lax.slice_in_dim(block, 0, width, axis=dim), axis, backward)
        block = jnp.concatenate([low, block, high], axis=dim)
    return block


def neighbour(values, stride, forward):
    cell_count = values.shape[-1]
    position = lax.iota(jnp.int32, cell_count) // stride % RES
    if forward:
        within = jnp.roll(values, -stride, axis=-1)
        wrapped = jnp.roll(values, (RES - 1) * stride, axis=-1)
        border = position == RES - 1
    else:
        within = jnp.roll(values, stride, axis=-1)
        wrapped = jnp.roll(values, (1 - RES) * stride, axis=-1)
        border = position == 0
    return jnp.where(border, wrapped, within)


def evaluate(
    potential_now,
    sensitivity,
    mean_field,
    permeability,
    grain_axes,
    thresholds,
    hyst_axis,
    hyst_weight,
):
    strides = (RES * RES, RES, 1)
    local_field = [
        mean_field[component] + neighbour(potential_now, strides[component], True) - potential_now
        for component in range(3)
    ]
    grain_field = [grain_axes[component] * local_field[component] for component in range(3)]
    magnet_sum = [0.0, 0.0, 0.0]
    pairs = [(0, 0), (0, 1), (0, 2), (1, 1), (1, 2), (2, 2)]
    stiff_sum = {pair: 0.0 for pair in pairs}
    for hysteron in range(NHYS):
        projection = (
            hyst_axis[0, hysteron] * grain_field[0]
            + hyst_axis[1, hysteron] * grain_field[1]
            + hyst_axis[2, hysteron] * grain_field[2]
        )
        switch = jnp.tanh(slope_gain * (projection - thresholds[hysteron]))
        slope_now = slope_gain * hyst_weight[hysteron] * (1.0 - switch * switch)
        for component in range(3):
            magnet_sum[component] = (
                magnet_sum[component]
                + hyst_weight[hysteron] * hyst_axis[component, hysteron] * switch
            )
        for pair in pairs:
            stiff_sum[pair] = (
                stiff_sum[pair]
                + hyst_axis[pair[0], hysteron] * hyst_axis[pair[1], hysteron] * slope_now
            )
    micro_flux = [
        permeability * (local_field[component] + grain_axes[component] * magnet_sum[component])
        for component in range(3)
    ]
    tangent_local = [
        [
            permeability
            * (
                grain_axes[left_comp]
                * grain_axes[right_comp]
                * stiff_sum[min(left_comp, right_comp), max(left_comp, right_comp)]
                + (1.0 if left_comp == right_comp else 0.0)
            )
            for right_comp in range(3)
        ]
        for left_comp in range(3)
    ]
    gradients = [
        [
            neighbour(sensitivity[column], strides[left_comp], True)
            - sensitivity[column]
            + (1.0 if left_comp == column else 0.0)
            for column in range(3)
        ]
        for left_comp in range(3)
    ]
    linear_flux = [
        [
            tangent_local[left_comp][0] * gradients[0][column]
            + tangent_local[left_comp][1] * gradients[1][column]
            + tangent_local[left_comp][2] * gradients[2][column]
            for column in range(3)
        ]
        for left_comp in range(3)
    ]
    return (micro_flux, tangent_local, linear_flux)


def divergence(fields):
    strides = (RES * RES, RES, 1)
    summed = fields[0] - neighbour(fields[0], strides[0], False)
    for component in (1, 2):
        summed = (
            summed + fields[component] - neighbour(fields[component], strides[component], False)
        )
    return summed


def micro_solve(
    potential_now, mean_field, thresholds, permeability, grain_axes, hyst_axis, hyst_weight
):
    strides = (RES * RES, RES, 1)
    sensitivity = [jnp.zeros_like(potential_now) for component in range(3)]
    for sweep_index in range(SWEEPS):
        micro_flux, tangent_local, linear_flux = evaluate(
            potential_now,
            sensitivity,
            mean_field,
            permeability,
            grain_axes,
            thresholds,
            hyst_axis,
            hyst_weight,
        )
        weight_sum = tangent_local[0][0]
        for left_comp in range(3):
            for right_comp in range(3):
                if left_comp + right_comp > 0:
                    weight_sum = weight_sum + tangent_local[left_comp][right_comp]
        for component in range(3):
            weight_sum = weight_sum + neighbour(
                tangent_local[component][component], strides[component], False
            )
        diagonal_sum = diag_boost * weight_sum
        potential_now = potential_now + divergence(micro_flux) / diagonal_sum
        sensitivity = [
            sensitivity[column]
            + divergence([linear_flux[component][column] for component in range(3)]) / diagonal_sum
            for column in range(3)
        ]
    micro_flux, tangent_local, linear_flux = evaluate(
        potential_now,
        sensitivity,
        mean_field,
        permeability,
        grain_axes,
        thresholds,
        hyst_axis,
        hyst_weight,
    )
    mean_flux = [jnp.mean(micro_flux[component], axis=-1) for component in range(3)]
    mean_tangent = [
        jnp.mean(linear_flux[left_comp][column], axis=-1)
        for left_comp in range(3)
        for column in range(3)
    ]
    return (potential_now, mean_flux, mean_tangent)


def make_thresholds(words, coerc, hyst_low, hyst_high):
    return [
        coerc
        * jnp.where(
            jnp.bitwise_and(jnp.right_shift(words, hysteron), 1) == 1,
            hyst_low[hysteron],
            hyst_high[hysteron],
        )
        for hysteron in range(NHYS)
    ]


def on_device(
    macro_field,
    rve_owner,
    potential,
    switch_words,
    permeability,
    coercivity,
    grain_axes,
    hyst_axis,
    hyst_low,
    hyst_high,
    hyst_weight,
    grad_weights,
    connectivity,
    node_order,
):
    groups = lax.axis_size("rve")
    points = potential.shape[0]
    cell_count = potential.shape[1]
    capacity = switch_words.shape[0] // groups
    slot_count = groups * capacity
    target = rve_owner[:, 0]
    owner_hits = (target[:, None] == lax.iota(jnp.int32, groups)[None, :]).astype(jnp.int32)
    earlier = jnp.cumsum(owner_hits, axis=0) - owner_hits
    rank_in = jnp.sum(earlier * owner_hits, axis=1)
    slot_of = target * capacity + rank_in
    placing = (lax.iota(jnp.int32, slot_count)[:, None] == slot_of[None, :]).astype(jnp.float32)
    send_phi = jnp.dot(placing, potential, precision=highest).reshape(groups, capacity, cell_count)
    send_field = jnp.einsum("sq,cq->sc", placing, macro_field, precision=highest).reshape(
        groups, capacity, 3
    )
    local_words = switch_words.reshape(groups, capacity, cell_count)
    local_perm = permeability.reshape(groups, capacity, cell_count)
    local_coerc = coercivity.reshape(groups, capacity, cell_count)
    local_grain = grain_axes.reshape(3, groups, capacity, cell_count)
    thresholds = make_thresholds(local_words, local_coerc, hyst_low, hyst_high)
    grain_list = [local_grain[component] for component in range(3)]
    recv_phi, recv_field = (
        lax.all_to_all(send_phi, "rve", split_axis=0, concat_axis=0, tiled=True),
        lax.all_to_all(send_field, "rve", split_axis=0, concat_axis=0, tiled=True),
    )
    mean_field = [recv_field[:, :, component][:, :, None] for component in range(3)]
    phi_new, mean_flux, mean_tangent = micro_solve(
        recv_phi, mean_field, thresholds, local_perm, grain_list, hyst_axis, hyst_weight
    )
    back_phi, back_flux, back_tangent = (
        lax.all_to_all(phi_new, "rve", split_axis=0, concat_axis=0, tiled=True),
        lax.all_to_all(
            jnp.stack(mean_flux, axis=-1), "rve", split_axis=0, concat_axis=0, tiled=True
        ),
        lax.all_to_all(
            jnp.stack(mean_tangent, axis=-1), "rve", split_axis=0, concat_axis=0, tiled=True
        ),
    )
    flux_point = jnp.einsum(
        "sq,sc->cq", placing, back_flux.reshape(slot_count, 3), precision=highest
    )
    nodal_terms = (
        grad_weights[0] * flux_point[0][None, :]
        + grad_weights[1] * flux_point[1][None, :]
        + grad_weights[2] * flux_point[2][None, :]
    )
    potential_new = jnp.einsum(
        "sq,sv->qv", placing, back_phi.reshape(slot_count, cell_count), precision=highest
    )
    tangent = jnp.einsum(
        "sq,sk->kq", placing, back_tangent.reshape(slot_count, 9), precision=highest
    ).reshape(3, 3, points)
    nodes_here = node_order.shape[0]
    matches = (connectivity[None, :, :] == lax.iota(jnp.int32, nodes_here)[:, None, None]).astype(
        jnp.float32
    )
    local_sum = jnp.einsum("naq,aq->n", matches, nodal_terms, precision=highest)
    structured = jnp.take(local_sum, node_order).reshape(EX + 1, EY + 1, EZ + 1)
    across = extended(structured, (("rve", 0),), 1)
    summed = structured.at[0].add(across[0]).at[EX].add(across[EX + 2])
    along_slab = extended(summed, (("slab", 1),), 1)
    node_total = summed.at[:, 0].add(along_slab[:, 0]).at[:, EY].add(along_slab[:, EY + 2])
    residual = jnp.zeros((nodes_here,), jnp.float32).at[node_order].set(node_total.reshape(-1))
    return (potential_new, tangent, residual)


def solution(mesh):
    return jax.shard_map(
        on_device,
        mesh=mesh,
        in_specs=(
            P(None, ("slab", "rve")),
            P(("slab", "rve"), None),
            P(("slab", "rve"), None),
            P(("slab", "rve"), None),
            P(("slab", "rve"), None),
            P(("slab", "rve"), None),
            P(None, ("slab", "rve"), None),
            P(),
            P(),
            P(),
            P(),
            P(None, None, ("slab", "rve")),
            P(None, ("slab", "rve")),
            P(("slab", "rve")),
        ),
        out_specs=(P(("slab", "rve"), None), P(None, None, ("slab", "rve")), P(("slab", "rve"))),
        check_vma=False,
    )
```

profile of v0, /device:TPU:1, one launch (start us, length us, event | category | flops | bytes accessed | tf_op | source)
XLA Modules:
  0.0 288.0 jit_solution(6554289289713035864)
XLA Ops:
  4.8 14.8 %all-to-all-start.1 = ((f32[64,4,3]{1,2,0:T(4,128)}), f32[64,4,3]{1,2,0:T(4,128)S(1)}, u32[]{:S(2)}, u32[]{:S(2)}) async-start(f32[64,4,3]{1,2,0:T(4,128)} %copy.41), calls=%async_computation.1 | async-start | bytes 262144 | tf_op jit(solution)/shard_map/all_to_all | solution.py:233
  23.7 6.4 %select_multiply_fusion.9 = (f32[256,512]{1,0:T(8,128)}, f32[256,512]{1,0:T(8,128)}, f32[256,512]{1,0:T(8,128)}, f32[256,512]{1,0:T(8,128)}) fusion(f32[256,512]{1,0:T(8,128)S(1)} %copy-done.31, s32[256,512]{1,0:T(8,128)S(1)} %copy-done.32, f32[]{:T(128)} %bitcast.9, f32[]{:T(128)} %bitcast.8, f32[]{:T(128)} %bitcast.21, f32[]{:T(128)} %bitcast.20, ...), kind=kLoop, calls=%fused_computation.240 | loop fusion | flops 2621440 | bytes 3145760 | tf_op jit(solution)/shard_map/mul | solution.py:184
  31.8 10.6 %all-to-all-start = ((f32[64,4,512]{2,1,0:T(4,128)}), f32[64,4,512]{2,1,0:T(4,128)S(1)}, u32[]{:S(2)}, u32[]{:S(2)}) async-start(f32[64,4,512]{2,1,0:T(4,128)} %reshape.330), calls=%async_computation | async-start | bytes 1048576 | tf_op jit(solution)/shard_map/all_to_all | solution.py:232
  91.6 2.2 reshape.340
  93.8 2.0 reshape.341
  102.4 10.3 %fusion.6 = (f32[64,4,512]{2,1,0:T(4,128)S(1)}, f32[64,4,512]{2,1,0:T(4,128)S(1)}, f32[64,4,512]{2,1,0:T(4,128)S(1)}, f32[64,4,512]{2,1,0:T(4,128)S(1)}, f32[64,...) fusion(f32[512]{0:T(512)S(1)} %get-tuple-element.195, ...), kind=kLoop, calls=%fused_computation.17 | loop fusion | flops 10354688 | bytes 11021424 | tf_op jit(solution)/shard_map/add | solution.py:111
  119.7 3.3 %fusion.82 = (f32[64,4,512]{2,1,0:T(4,128)S(1)}, f32[64,4,512]{2,1,0:T(4,128)S(1)}) fusion(f32[64,4,512]{2,1,0:T(4,128)S(1)} %get-tuple-element.110, f32[64,4,512]{2,1,0:T(4,128)S(1)} %get-tuple-element.106, f32[64,4,512]{2,1,0:T(4,128)S(1)} %get-tuple-element.96, f32[64,4,448]{2,1,0:T(4,128)S(1)} %bitcast.269, f32[64,4,64]{2,1,0:T(4,128)S(1)} %slice.1534, ...), kind=kLoop, calls=%fused_computation.139 | loop fusion | flops 4194304 | bytes 11011072 | tf_op jit(solution)/shard_map/div | solution.py:160
  128.4 11.1 %multiply_add_fusion.2 = (f32[64,4,512]{2,1,0:T(4,128)S(1)}, f32[64,4,512]{2,1,0:T(4,128)S(1)}, f32[64,4,512]{2,1,0:T(4,128)S(1)}, f32[64,4,512]{2,1,0:T(4,128)S...) fusion(f32[64,4,512]{2,1,0:T(4,128)S(1)} %get-tuple-element.94,, ...), kind=kLoop, calls=%fused_computation.177 | loop fusion | flops 11141120 | bytes 14681200 | tf_op jit(solution)/shard_map/add | solution.py:111
  146.3 3.0 %fusion.94 = (f32[64,4,512]{2,1,0:T(4,128)S(1)}, f32[64,4,512]{2,1,0:T(4,128)S(1)}) fusion(f32[64,4,512]{2,1,0:T(4,128)S(1)} %get-tuple-element.94, f32[64,4,511]{2,1,0:T(4,128)S(1)} %bitcast.220, f32[64,4,1]{2,1,0:T(4,128)S(1)} %slice.1562, f32[64,4,7]{2,1,0:T(4,128)S(1)} %slice.1561, f32[64,4,505]{2,1,0:T(4,128)S(1)} %slice.1560, ...), kind=kLoop, calls=%fused_computation.242 | loop fusion | flops 4325376 | bytes 11535360 | tf_op jit(solution)/shard_map/add | solution.py:159
  186.6 2.9 fusion.137
  189.5 10.2 %multiply_reduce_fusion.2 = (f32[64,4]{1,0:T(8,128)S(1)}, f32[64,4,512]{2,1,0:T(4,128)S(1)}, f32[64,4,512]{2,1,0:T(4,128)S(1)}, f32[64,4,512]{2,1,0:T(4,128)S(1)}, f32[64,4,512]{2,1,0:T(4,128)S(1)}) fusion(f32[64,4,512]{2,1,0:T(4,128)S(1)} %reshape.331, f32[64,4,512]{2,1,0:T(4,128)S(1)} %squeeze.63, f32[]{:T(128)S(6)} %mul.1571, f32[]{:T(128)S(6)} %mul.1560, ...), kind=kLoop, calls=%fused_computation.164 | loop fusion | flops 5504768 | bytes 7866432 | tf_op jit(solution)/shard_map/reduce_sum | solution.py:173
  199.7 2.1 add_multiply_fusion.2
  201.8 2.0 multiply_multiply_fusion.1
  213.2 2.0 add_multiply_fusion.1
  217.0 10.9 %all-to-all-start.4 = ((f32[64,4,3]{1,2,0:T(4,128)}), f32[64,4,3]{1,2,0:T(4,128)}, u32[]{:S(2)}, u32[]{:S(2)}) async-start(f32[64,4,3]{1,2,0:T(4,128)} %copy.44), calls=%async_computation.4 | async-start | bytes 262144 | tf_op jit(solution)/shard_map/all_to_all | solution.py:241
  228.0 2.6 maximum_subtract_fusion.13
  233.9 3.8 %add_reduce_fusion.2 = (f32[64,4]{1,0:T(8,128)S(1)}, f32[64,4]{1,0:T(8,128)S(1)}, f32[64,4]{1,0:T(8,128)S(1)}, f32[64,4]{1,0:T(8,128)S(1)}, f32[64,4]{1,0:T(8,12...) fusion(f32[64,4,512]{2,1,0:T(4,128)S(1)} %copy-done.13, ...), kind=kLoop, calls=%fused_computation.167 | loop fusion | flops 7075584 | bytes 7873536 | tf_op jit(solution)/shard_map/reduce_sum | solution.py:175
  239.0 10.3 %all-to-all-start.3 = ((f32[64,4,9]{2,1,0:T(4,128)}), f32[64,4,9]{2,1,0:T(4,128)S(1)}, u32[]{:S(2)}, u32[]{:S(2)}) async-start(f32[64,4,9]{2,1,0:T(4,128)} %copy.42), calls=%async_computation.3 | async-start | bytes 262144 | tf_op jit(solution)/shard_map/all_to_all | solution.py:244
  251.8 3.5 %collective-permute-start = (f32[1,3,5]{2,1,0:T(4,128)S(1)}, f32[1,3,5]{2,1,0:T(4,128)S(1)}, u32[]{:S(2)}, u32[]{:S(2)}) collective-permute-start(f32[1,3,5]{2,1,0:T(4,128)S(1)} %slice.1374), channel_id=1, source_target_pairs={{0,1},{1,2},{2,3},{3,4},{4,5},{5,6},{6,7},{7,8},{8,9},{9,10},{10,1... | collective-permute-start | bytes 188 | tf_op jit(solution)/shard_map/ppermute | solution.py:24
  257.3 2.4 all-to-all-done.3
  259.7 9.3 %all-to-all-start.2 = ((f32[64,4,512]{2,1,0:T(4,128)}), f32[64,4,512]{2,1,0:T(4,128)S(1)}, u32[]{:S(2)}, u32[]{:S(2)}) async-start(f32[64,4,512]{2,1,0:T(4,128)} %fusion.97), calls=%async_computation.2 | async-start | bytes 1048576 | tf_op jit(solution)/shard_map/all_to_all | solution.py:240
  269.1 3.2 %collective-permute-start.2 = (f32[3,1,5]{2,1,0:T(1,128)S(1)}, f32[3,1,5]{2,1,0:T(1,128)S(1)}, u32[]{:S(2)}, u32[]{:S(2)}) collective-permute-start(f32[3,1,5]{2,1,0:T(1,128)S(1)} %slice.1576), channel_id=1, source_target_pairs={{0,64},{64,128},{128,192},{192,256},{256,320},{320,384},{384,448},... | collective-permute-start | bytes 188 | tf_op jit(solution)/shard_map/ppermute | solution.py:24
  274.3 3.8 %collective-permute-done.3 = f32[3,1,5]{2,1,0:T(1,128)S(1)} collective-permute-done((f32[3,1,5]{2,1,0:T(1,128)S(1)}, f32[3,1,5]{2,1,0:T(1,128)S(1)}, u32[]{:S(2)}, u32[]{:S(2)}) %collective-permute-start.3) | collective-permute-done | bytes 92 | tf_op jit(solution)/shard_map/ppermute | solution.py:27
  280.4 5.9 %all-to-all-done.2 = f32[64,4,512]{2,1,0:T(4,128)S(1)} async-done(((f32[64,4,512]{2,1,0:T(4,128)}), f32[64,4,512]{2,1,0:T(4,128)S(1)}, u32[]{:S(2)}, u32[]{:S(2)}) %all-to-all-start.2) | async-done | bytes 524320 | tf_op jit(solution)/shard_map/all_to_all | solution.py:240
  (336 shorter events, 99.0 us)
Async XLA Ops:
  0.6 19.0 %copy-start = (f32[128,512]{1,0:T(8,128)S(1)}, f32[128,512]{1,0:T(8,128)}, u32[]{:S(2)}) copy-start(f32[128,512]{1,0:T(8,128)} %param.24) | copy-start | bytes 786436
  4.8 26.9 %all-to-all-start.1 = ((f32[64,4,3]{1,2,0:T(4,128)}), f32[64,4,3]{1,2,0:T(4,128)S(1)}, u32[]{:S(2)}, u32[]{:S(2)}) async-start(f32[64,4,3]{1,2,0:T(4,128)} %copy.41), calls=%async_computation.1 | async-start | bytes 262144 | tf_op jit(solution)/shard_map/all_to_all | solution.py:233
  20.1 3.0 %copy-start.37 = (f32[4]{0:T(128)S(1)}, f32[4]{0:T(128)}, u32[]{:S(2)}) copy-start(f32[4]{0:T(128)} %param.31) | copy-start | bytes 52
  20.1 3.6 %copy-start.31 = (f32[256,512]{1,0:T(8,128)S(1)}, f32[256,512]{1,0:T(8,128)}, u32[]{:S(2)}) copy-start(f32[256,512]{1,0:T(8,128)} %param.27) | copy-start | bytes 1572868
  20.1 3.6 %copy-start.32 = (s32[256,512]{1,0:T(8,128)S(1)}, s32[256,512]{1,0:T(8,128)}, u32[]{:S(2)}) copy-start(s32[256,512]{1,0:T(8,128)} %param.25) | copy-start | bytes 1572868
  23.7 6.5 %copy-start.38 = (f32[4]{0:T(128)S(1)}, f32[4]{0:T(128)}, u32[]{:S(2)}) copy-start(f32[4]{0:T(128)} %param.32) | copy-start | bytes 52
  31.8 67.6 %all-to-all-start = ((f32[64,4,512]{2,1,0:T(4,128)}), f32[64,4,512]{2,1,0:T(4,128)S(1)}, u32[]{:S(2)}, u32[]{:S(2)}) async-start(f32[64,4,512]{2,1,0:T(4,128)} %reshape.330), calls=%async_computation | async-start | bytes 1048576 | tf_op jit(solution)/shard_map/all_to_all | solution.py:232
  90.4 5.5 %copy-start.20 = (f32[256,512]{1,0:T(8,128)S(1)}, f32[256,512]{1,0:T(8,128)}, u32[]{:S(2)}) copy-start(f32[256,512]{1,0:T(8,128)} %get-tuple-element.160) | copy-start | bytes 1572868
  91.6 36.8 %copy-start.4 = (f32[64,4,512]{2,1,0:T(4,128)}, f32[64,4,512]{2,1,0:T(4,128)S(1)}, u32[]{:S(2)}) copy-start(f32[64,4,512]{2,1,0:T(4,128)S(1)} %reshape.339) | copy-start | bytes 1572868
  93.8 4.3 %copy-start.41 = (s32[45]{0:T(128)S(1)}, s32[45]{0:T(128)}, u32[]{:S(2)}) copy-start(s32[45]{0:T(128)} %param.35) | copy-start | bytes 544
  93.8 4.8 %copy-start.39 = (s32[8,128]{1,0:T(8,128)S(1)}, s32[8,128]{1,0:T(8,128)}, u32[]{:S(2)}) copy-start(s32[8,128]{1,0:T(8,128)} %param.34) | copy-start | bytes 12292
  179.5 6.4 %copy-start.2 = (f32[64,4,512]{2,1,0:T(4,128)}, f32[64,4,512]{2,1,0:T(4,128)S(1)}, u32[]{:S(2)}) copy-start(f32[64,4,512]{2,1,0:T(4,128)S(1)} %fusion.95) | copy-start | bytes 1572868
  186.6 2.9 %copy-start.5 = (f32[64,4,512]{2,1,0:T(4,128)S(1)}, f32[64,4,512]{2,1,0:T(4,128)}, u32[]{:S(2)}) copy-start(f32[64,4,512]{2,1,0:T(4,128)} %copy-done.4) | copy-start | bytes 1572868
  217.0 22.0 %all-to-all-start.4 = ((f32[64,4,3]{1,2,0:T(4,128)}), f32[64,4,3]{1,2,0:T(4,128)}, u32[]{:S(2)}, u32[]{:S(2)}) async-start(f32[64,4,3]{1,2,0:T(4,128)} %copy.44), calls=%async_computation.4 | async-start | bytes 262144 | tf_op jit(solution)/shard_map/all_to_all | solution.py:241
  237.7 12.8 %copy-start.35 = (f32[3,8,128]{2,1,0:T(8,128)S(1)}, f32[3,8,128]{2,1,0:T(8,128)}, u32[]{:S(2)}) copy-start(f32[3,8,128]{2,1,0:T(8,128)} %param.33) | copy-start | bytes 36868
  237.7 12.8 %copy-start.33 = (pred[45,8,128]{2,1,0:T(8,128)(4,1)S(1)}, pred[45,8,128]{2,1,0:T(8,128)(4,1)}, u32[]{:S(2)}) copy-start(pred[45,8,128]{2,1,0:T(8,128)(4,1)} %iota_compare_fusion) | copy-start | bytes 138244
  237.7 13.8 %copy-start.42 = (s32[45]{0:T(128)S(1)}, s32[45]{0:T(128)}, u32[]{:S(2)}) copy-start(s32[45]{0:T(128)} %param.35) | copy-start | bytes 544
  239.0 20.7 %all-to-all-start.3 = ((f32[64,4,9]{2,1,0:T(4,128)}), f32[64,4,9]{2,1,0:T(4,128)S(1)}, u32[]{:S(2)}, u32[]{:S(2)}) async-start(f32[64,4,9]{2,1,0:T(4,128)} %copy.42), calls=%async_computation.3 | async-start | bytes 262144 | tf_op jit(solution)/shard_map/all_to_all | solution.py:244
  251.8 17.2 %collective-permute-start = (f32[1,3,5]{2,1,0:T(4,128)S(1)}, f32[1,3,5]{2,1,0:T(4,128)S(1)}, u32[]{:S(2)}, u32[]{:S(2)}) collective-permute-start(f32[1,3,5]{2,1,0:T(4,128)S(1)} %slice.1374), channel_id=1, source_target_pairs={{0,1},{1,2},{2,3},{3,4},{4,5},{5,6},{6,7},{7,8},{8,9},{9,10},{10,1... | collective-permute-start | bytes 188 | tf_op jit(solution)/shard_map/ppermute | solution.py:24
  255.3 32.3 %copy-start.1 = (f32[128,512]{1,0:T(8,128)S(1)}, f32[128,512]{1,0:T(8,128)}, u32[]{:S(2)}) copy-start(f32[128,512]{1,0:T(8,128)} %param.24) | copy-start | bytes 786436
  255.4 13.6 %collective-permute-start.1 = (f32[1,3,5]{2,1,0:T(4,128)S(1)}, f32[1,3,5]{2,1,0:T(4,128)S(1)}, u32[]{:S(2)}, u32[]{:S(2)}) collective-permute-start(f32[1,3,5]{2,1,0:T(4,128)S(1)} %reshape.337), channel_id=1, source_target_pairs={{1,0},{2,1},{3,2},{4,3},{5,4},{6,5},{7,6},{8,7},{9,8},{10,9},{11,1... | collective-permute-start | bytes 188 | tf_op jit(solution)/shard_map/ppermute | solution.py:27
  259.7 26.6 %all-to-all-start.2 = ((f32[64,4,512]{2,1,0:T(4,128)}), f32[64,4,512]{2,1,0:T(4,128)S(1)}, u32[]{:S(2)}, u32[]{:S(2)}) async-start(f32[64,4,512]{2,1,0:T(4,128)} %fusion.97), calls=%async_computation.2 | async-start | bytes 1048576 | tf_op jit(solution)/shard_map/all_to_all | solution.py:240
  269.1 3.9 %collective-permute-start.2 = (f32[3,1,5]{2,1,0:T(1,128)S(1)}, f32[3,1,5]{2,1,0:T(1,128)S(1)}, u32[]{:S(2)}, u32[]{:S(2)}) collective-permute-start(f32[3,1,5]{2,1,0:T(1,128)S(1)} %slice.1576), channel_id=1, source_target_pairs={{0,64},{64,128},{128,192},{192,256},{256,320},{320,384},{384,448},... | collective-permute-start | bytes 188 | tf_op jit(solution)/shard_map/ppermute | solution.py:24
  273.0 5.1 %collective-permute-start.3 = (f32[3,1,5]{2,1,0:T(1,128)S(1)}, f32[3,1,5]{2,1,0:T(1,128)S(1)}, u32[]{:S(2)}, u32[]{:S(2)}) collective-permute-start(f32[3,1,5]{2,1,0:T(1,128)S(1)} %get-tuple-element.189), channel_id=1, source_target_pairs={{64,0},{128,64},{192,128},{256,192},{320,256},{384,320},{448,384},... | collective-permute-start | bytes 188 | tf_op jit(solution)/shard_map/ppermute | solution.py:27
  (28 other events, 51.2 us)
where the time goes:
time: 293 us; the launch traced here: 288 us
  other arithmetic  87.6 us (30%)
  local copies, waits for them, and re-layouts  68.1 us (23%)
  starting transfers between devices  66 us (23%)
  between operations  50.2 us (17%)
  waiting for transfers between devices  12.8 us (4%)
  matrix products  3.33 us (1%)
    add x10, other arithmetic, evaluate(): tangent_local[left_comp][0] * gradients[0][column]  30 us
    slice x38, local copies, waits for them, and re-layouts, neighbour(): within = jnp.roll(values, -stride, axis=-1)  19.2 us
    slice x39, local copies, waits for them, and re-layouts, neighbour(): wrapped = jnp.roll(values, (RES - 1) * stride, axis=-1)  16.3 us
    all_to_all x1, starting transfers between devices, on_device(): lax.all_to_all(send_field, 'rve', split_axis=0, concat_axis=0, tiled=True)  14.8 us
    reduce_sum x2, other arithmetic, micro_solve(): jnp.mean(micro_flux[component], axis=-1)  11.3 us
    all_to_all x1, starting transfers between devices, on_device(): lax.all_to_all(jnp.stack(mean_flux, axis=-1), 'rve', split_axis=0, concat...  10.9 us
    all_to_all x1, starting transfers between devices, on_device(): lax.all_to_all(send_phi, 'rve', split_axis=0, concat_axis=0, tiled=True)  10.6 us
    all_to_all x1, starting transfers between devices, on_device(): lax.all_to_all(jnp.stack(mean_tangent, axis=-1), 'rve', split_axis=0, con...  10.3 us
  transfers between devices with their start and end apart: 9, of which 4 were waited for; matrix products, arithmetic and copies ran while one was open for 12% of the time, Pallas kernels for 0%

commit v1 on v0

v1 whole, which is shorter than its diff:
```python
import jax
import jax.numpy as jnp
from jax import lax
from jax.experimental import pallas as pl
from jax.experimental.pallas import tpu as pltpu
from jax.sharding import PartitionSpec as P

MESH = pl.DeviceIdType.MESH
f32 = jnp.float32
bf16 = jnp.bfloat16

GROUPS = 4
PEERS = 16
CAP = 4
SLOTS = PEERS * CAP
RVES = GROUPS * PEERS
SLABS = 8
PTS = 128
HALF = 256
NODES = 45

PERM = 0
GRAIN = 1
TH = 4
PG = 8
AIJ = 11
PHI = 17
PSI = 20
COER = 26
N_FIELDS = 27
PAIRS = ((0, 0), (0, 1), (0, 2), (1, 1), (1, 2), (2, 2))


def iota(shape, dim):
    return lax.broadcasted_iota(jnp.int32, shape, dim)


def dot(a, b):
    return lax.dot_general(a, b, (((1,), (0,)), ((), ())), precision=lax.Precision.HIGHEST,
                           preferred_element_type=f32)


def dot_t(a, b):
    return lax.dot_general(a, b, (((1,), (1,)), ((), ())), precision=lax.Precision.HIGHEST,
                           preferred_element_type=f32)


def pick(hot, data):
    hot = hot.astype(bf16)
    high = data.astype(bf16)
    low = (data - high.astype(f32)).astype(bf16)
    one = lax.dot_general(hot, high, (((1,), (0,)), ((), ())), preferred_element_type=f32)
    two = lax.dot_general(hot, low, (((1,), (0,)), ((), ())), preferred_element_type=f32)
    return one + two


def swap(v):
    return pltpu.roll(v, 64, v.ndim - 1)


def next_x(v):
    return jnp.concatenate([v[1:], swap(v[:1])], axis=0)


def prev_x(v):
    return jnp.concatenate([swap(v[3:]), v[:3]], axis=0)


def next_z(v):
    return pltpu.roll(v, 7, 1)


def prev_z(v):
    return pltpu.roll(v, 1, 1)


def recip(v):
    r = pl.reciprocal(v, approx=True)
    return r * (2.0 - v * r)


def sum_x(v):
    return (v[0] + v[1]) + (v[2] + v[3])


def to_rows(recv):
    n = recv.shape[-1]
    pairs = recv.reshape(8, 2, 8, n)
    even, odd = pairs[:, 0], pairs[:, 1]
    first = iota((8, 8, n), 1) < 4
    low = jnp.where(first, even, pltpu.roll(odd, 4, 1))
    high = jnp.where(first, pltpu.roll(even, 4, 1), odd)
    return jnp.concatenate([low.reshape(64, n), high.reshape(64, n)], axis=0)


def kernel(
    owner_ref, macro_ref, pot_ref, words_hbm, perm_hbm, coer_hbm, grain_hbm,
    axis_ref, low_ref, high_ref, weight_ref, gw_ref, conn_ref, order_ref,
    pot_out, tan_out, res_out,
    nat_words, nat_perm, nat_coer, nat_grain, words_t, fields,
    send_phi, send_mac, recv_phi, recv_mac, ret_phi, ret_val, back_phi, back_val,
    acc_ref, halo_src, halo_dst,
    load_sem, out_phi_send, out_phi_recv, out_mac_send, out_mac_recv,
    ret_phi_send, ret_phi_recv, ret_val_send, ret_val_recv, halo_send, halo_recv,
):
    me = lax.axis_index("rve")
    slab = lax.axis_index("slab")
    my_x = lax.div(me, PEERS)
    my_low = lax.rem(me, PEERS)
    right, left = lax.rem(me + 1, RVES), lax.rem(me + RVES - 1, RVES)
    above, below = lax.rem(slab + 1, SLABS), lax.rem(slab + SLABS - 1, SLABS)

    barrier = pltpu.get_barrier_semaphore()

    def greet(i, carry):
        peer = lax.rem(me + i, RVES)
        pl.semaphore_signal(barrier, inc=1, device_id=(slab, peer), device_id_type=MESH)
        return carry

    lax.fori_loop(1, RVES, greet, 0)
    for s in (above, below):
        for r in (left, me, right):
            pl.semaphore_signal(barrier, inc=1, device_id=(s, r), device_id_type=MESH)

    def loads(t):
        rows = pl.ds(lax.rem(my_x - t + GROUPS, GROUPS) * SLOTS, SLOTS)
        return (
            pltpu.make_async_copy(words_hbm.at[rows], nat_words.at[t], load_sem.at[0, t]),
            pltpu.make_async_copy(perm_hbm.at[rows], nat_perm.at[t], load_sem.at[1, t]),
            pltpu.make_async_copy(coer_hbm.at[rows], nat_coer.at[t], load_sem.at[2, t]),
            pltpu.make_async_copy(grain_hbm.at[:, rows], nat_grain.at[t], load_sem.at[3, t]),
        )

    for t in range(GROUPS):
        for copy in loads(t):
            copy.start()

    target_row = owner_ref[...]
    target_rows = jnp.broadcast_to(target_row.astype(f32), (PTS, PTS))
    target_cols = target_rows.T
    same = target_rows == target_cols
    q_row, q_col = iota((PTS, PTS), 1), iota((PTS, PTS), 0)
    rank_row = jnp.sum(jnp.where(same & (q_col < q_row), 1.0, 0.0), axis=0, keepdims=True).astype(jnp.int32)
    rank_col = jnp.sum(jnp.where(same & (q_row < q_col), 1.0, 0.0), axis=1, keepdims=True).astype(jnp.int32)
    target_col = target_cols[:, :1].astype(jnp.int32)
    place_row = target_row * 8 + rank_row
    place_col = target_col * 8 + rank_col

    slot_rows = iota((RVES * 8, PTS), 0)
    hot = jnp.concatenate([(slot_rows == place_row).astype(f32), (slot_rows == place_row + 4).astype(f32)], axis=1)
    halves = jnp.concatenate([pot_ref[:, :HALF], pot_ref[:, HALF:]], axis=0)
    send_phi[...] = pick(hot, halves).reshape(RVES, 8, HALF)

    n_rows = iota((PTS, PTS), 0)
    comp = n_rows // CAP
    spread = jnp.where(comp == 0, macro_ref[0:1], jnp.where(comp == 1, macro_ref[1:2], macro_ref[2:3]))
    spread = jnp.where((comp < 3) & (n_rows % CAP == rank_row), spread, 0.0)
    owner_hot = (iota((RVES, PTS), 0) == target_row).astype(f32)
    send_mac[...] = dot_t(owner_hot, spread).reshape(RVES, 1, PTS)

    pl.semaphore_wait(barrier, RVES - 1 + 6)

    def send(t):
        peer_x = lax.rem(my_x + t, GROUPS)

        def one(i, carry):
            peer = peer_x * PEERS + lax.rem(my_low + i, PEERS)

            @pl.when(peer != me)
            def _():
                pltpu.make_async_remote_copy(
                    src_ref=send_phi.at[peer], dst_ref=recv_phi.at[t, my_low],
                    send_sem=out_phi_send.at[t], recv_sem=out_phi_recv.at[t],
                    device_id=(slab, peer), device_id_type=MESH).start()
                pltpu.make_async_remote_copy(
                    src_ref=send_mac.at[peer], dst_ref=recv_mac.at[t, my_low],
                    send_sem=out_mac_send.at[t], recv_sem=out_mac_recv.at[t],
                    device_id=(slab, peer), device_id_type=MESH).start()

            @pl.when(peer == me)
            def _():
                pltpu.make_async_copy(send_phi.at[peer], recv_phi.at[t, my_low], out_phi_recv.at[t]).start()
                pltpu.make_async_copy(send_mac.at[peer], recv_mac.at[t, my_low], out_mac_recv.at[t]).start()

            return carry

        lax.fori_loop(0, PEERS, one, 0)

    for t in range(GROUPS):
        send(t)

    lane_peer = iota((PTS, PEERS), 0) // CAP % PEERS
    peer_t = (lane_peer == iota((PTS, PEERS), 1)).astype(f32)
    peer_m = (iota((PEERS, PTS), 1) // CAP % PEERS == iota((PEERS, PTS), 0)).astype(f32)
    mask_mac = iota((PTS, PTS), 0) % CAP == iota((PTS, PTS), 1) % CAP
    comp_m = (iota((8, PTS), 1) // CAP == iota((8, PTS), 0)).astype(f32)
    val_n = iota((PTS, 96), 0) % 32
    val_k = iota((PTS, 96), 1) // 8
    val_hot = jnp.where(
        jnp.where(val_k < 3, val_k, (val_k // 3) * 8 + val_k % 3) == val_n, 1.0 / 512.0, 0.0)
    mask_val = iota((PTS, PTS), 0) // 32 == iota((PTS, PTS), 1) % CAP

    axis2 = [[2.0 * axis_ref[c, k] for k in range(4)] for c in range(3)]
    mag_w = [[weight_ref[k] * axis_ref[c, k] for k in range(4)] for c in range(3)]
    pair_w = [[2.0 * weight_ref[k] * axis_ref[a, k] * axis_ref[b, k] for k in range(4)] for a, b in PAIRS]
    low2 = [2.0 * low_ref[k] for k in range(4)]
    high2 = [2.0 * high_ref[k] for k in range(4)]

    def evaluate(y, version, mean):
        now = fields[PHI + version, :, y]
        y_next = fields[PHI + version, :, lax.rem(y + 1, 8)]
        h = [mean[0] + (next_x(now) - now), mean[1] + (y_next - now), mean[2] + (next_z(now) - now)]
        g = [fields[GRAIN + c, :, y] * h[c] for c in range(3)]
        s = []
        for k in range(4):
            arg = axis2[0][k] * g[0] + axis2[1][k] * g[1] + axis2[2][k] * g[2] - fields[TH + k, :, y]
            s.append(jnp.tanh(arg))
        slope = [1.0 - v * v for v in s]
        perm = fields[PERM, :, y]
        flux = []
        for c in range(3):
            mag = mag_w[c][0] * s[0] + mag_w[c][1] * s[1] + mag_w[c][2] * s[2] + mag_w[c][3] * s[3]
            flux.append(perm * h[c] + fields[PG + c, :, y] * mag)
        stiff = {}
        for i, pair in enumerate(PAIRS):
            w = pair_w[i]
            total = w[0] * slope[0] + w[1] * slope[1] + w[2] * slope[2] + w[3] * slope[3]
            v = fields[AIJ + i, :, y] * total
            if pair[0] == pair[1]:
                v = v + perm
            stiff[pair] = v
            stiff[pair[::-1]] = v
        return now, flux, stiff

    def sweep_body(y, first, mean, carry):
        now, flux, stiff = evaluate(y, 0 if first else 1, mean)
        if first:
            lin = stiff
        else:
            lin = {}
            psi = [fields[PSI + d, :, y] for d in range(3)]
            psi_y = [fields[PSI + d, :, lax.rem(y + 1, 8)] for d in range(3)]
            for d in range(3):
                grad = [next_x(psi[d]) - psi[d], psi_y[d] - psi[d], next_z(psi[d]) - psi[d]]
                grad[d] = grad[d] + 1.0
                for c in range(3):
                    lin[c, d] = stiff[c, 0] * grad[0] + stiff[c, 1] * grad[1] + stiff[c, 2] * grad[2]
        nxt = (flux[1], stiff[1, 1], lin[1, 0], lin[1, 1], lin[1, 2])
        cross = stiff[0, 1] + stiff[0, 2] + stiff[1, 2]
        weight = (stiff[0, 0] + stiff[1, 1] + stiff[2, 2] + (cross + cross)
                  + prev_x(stiff[0, 0]) + prev_z(stiff[2, 2]))
        force = (flux[0] - prev_x(flux[0])) + flux[1] + (flux[2] - prev_z(flux[2]))
        forces = [(lin[0, d] - prev_x(lin[0, d])) + lin[1, d] + (lin[2, d] - prev_z(lin[2, d])) for d in range(3)]
        if carry is not None:
            force, weight, forces = close(force, weight, forces, carry)
        return nxt, (force, weight, forces)

    def close(force, weight, forces, carry):
        return force - carry[0], weight + carry[1], [forces[d] - carry[2 + d] for d in range(3)]

    def apply(y, first, sums):
        force, weight, forces = sums
        inv = recip(1.5 * weight)
        old, new = (0, 1) if first else (1, 2)
        fields[PHI + new, :, y] = fields[PHI + old, :, y] + force * inv
        for d in range(3):
            step = forces[d] * inv
            if not first:
                step = fields[PSI + d, :, y] + step
            fields[PSI + (0 if first else 3) + d, :, y] = step

    def sweep(first, mean):
        carry, (force, weight, forces) = sweep_body(0, first, mean, None)

        def step(y, carry):
            nxt, sums = sweep_body(y, first, mean, carry)
            apply(y, first, sums)
            return nxt

        carry = lax.fori_loop(1, 8, step, carry)
        apply(0, first, close(force, weight, forces, carry))

    def last(mean):
        def step(y, carry):
            prev, acc = carry
            now, flux, stiff = evaluate(y, 2, mean)
            psi = [fields[PSI + 3 + d, :, y] for d in range(3)]
            acc = list(acc)
            for c in range(3):
                acc[c] = acc[c] + sum_x(flux[c])
            for i, pair in enumerate(PAIRS):
                acc[3 + i] = acc[3 + i] + sum_x(stiff[pair])
            for c in range(3):
                div = ((stiff[0, c] - prev_x(stiff[0, c])) + (stiff[1, c] - prev[c])
                       + (stiff[2, c] - prev_z(stiff[2, c])))
                for d in range(3):
                    acc[9 + 3 * c + d] = acc[9 + 3 * c + d] + sum_x(div * psi[d])
            return (stiff[0, 1], stiff[1, 1], stiff[1, 2]), tuple(acc)

        zero = jnp.zeros((4, 8, PTS), f32)
        flat = jnp.zeros((8, PTS), f32)
        prev, acc = lax.fori_loop(0, 8, step, ((zero,) * 3, (flat,) * 18))
        psi = [fields[PSI + 3 + d, :, 0] for d in range(3)]
        for c in range(3):
            acc_ref[8 * c:8 * c + 8] = acc[c]
            for d in range(3):
                pair = PAIRS.index((min(c, d), max(c, d)))
                k = 3 + 3 * c + d
                acc_ref[8 * k:8 * k + 8] = acc[3 + pair] - acc[9 + 3 * c + d] + sum_x(prev[c] * psi[d])

    def turn(nat, h):
        a = nat[:, h * PTS:(h + 1) * PTS]
        b = nat[:, HALF + h * PTS:HALF + (h + 1) * PTS]
        return jnp.concatenate([a, b], axis=0).T.reshape(2, 8, 8, PTS)

    def group(t, carry):
        for copy in loads(t):
            copy.wait()
        for h in range(2):
            xs = slice(2 * h, 2 * h + 2)
            words_t[xs] = turn(nat_words[t], h)
            fields[COER, xs] = turn(nat_coer[t], h)
            fields[PERM, xs] = turn(nat_perm[t], h)
            for c in range(3):
                fields[GRAIN + c, xs] = turn(nat_grain[t, c], h)

        def prepare(y, carry):
            words = words_t[:, y]
            coer = fields[COER, :, y]
            for k in range(4):
                up = jnp.bitwise_and(words, 1 << k) != 0
                fields[TH + k, :, y] = coer * jnp.where(up, low2[k], high2[k])
            perm = fields[PERM, :, y]
            grain = [fields[GRAIN + c, :, y] for c in range(3)]
            pg = [perm * grain[c] for c in range(3)]
            for c in range(3):
                fields[PG + c, :, y] = pg[c]
            for i, (a, b) in enumerate(PAIRS):
                fields[AIJ + i, :, y] = pg[a] * grain[b]
            return carry

        lax.fori_loop(0, 8, prepare, 0)

        pltpu.make_async_copy(recv_phi.at[t], recv_phi.at[t], out_phi_recv.at[t]).wait()
        pltpu.make_async_copy(recv_mac.at[t], recv_mac.at[t], out_mac_recv.at[t]).wait()
        rows = to_rows(recv_phi[t])
        for h in range(2):
            fields[PHI, 2 * h:2 * h + 2] = rows[:, h * PTS:(h + 1) * PTS].T.reshape(2, 8, 8, PTS)
        mac = dot(peer_t, recv_mac[t, :, 0, :])
        mac = dot_t(comp_m, jnp.where(mask_mac, mac, 0.0))
        mean = [jnp.broadcast_to(mac[c:c + 1], (8, PTS))[None] for c in range(3)]

        sweep(True, mean)
        sweep(False, mean)

        first = iota((8, 8, PTS), 1) < 4
        for h in range(2):
            block = fields[PHI + 2, 2 * h:2 * h + 2].reshape(PTS, PTS).T.reshape(2, 8, 8, PTS)
            low, high = block[0], block[1]
            cols = slice(h * PTS, (h + 1) * PTS)
            ret_phi[t, :, 0, :, cols] = jnp.where(first, low, pltpu.roll(high, 4, 1))
            ret_phi[t, :, 1, :, cols] = jnp.where(first, pltpu.roll(low, 4, 1), high)

        src_x = lax.rem(my_x - t + GROUPS, GROUPS)

        def give(src, dst, send_sem, recv_sem):
            def one(i, carry):
                low = lax.rem(my_low + i, PEERS)
                peer = src_x * PEERS + low
                piece = src(low)

                @pl.when(peer != me)
                def _():
                    pltpu.make_async_remote_copy(
                        src_ref=piece, dst_ref=dst.at[me], send_sem=send_sem.at[t], recv_sem=recv_sem.at[t],
                        device_id=(slab, peer), device_id_type=MESH).start()

                @pl.when(peer == me)
                def _():
                    pltpu.make_async_copy(piece, dst.at[me], recv_sem.at[t]).start()

                return carry

            lax.fori_loop(0, PEERS, one, 0)

        give(lambda low: ret_phi.at[t, lax.div(low, 2), lax.rem(low, 2)], back_phi, ret_phi_send, ret_phi_recv)
        last(mean)
        val = jnp.where(mask_val, dot(val_hot, acc_ref[...]), 0.0)
        ret_val[t] = dot_t(peer_m, val).reshape(PEERS, 1, PTS)
        give(lambda low: ret_val.at[t, low], back_val, ret_val_send, ret_val_recv)
        return carry

    lax.fori_loop(0, GROUPS, group, 0)

    for t in range(GROUPS):
        mine = back_val.at[pl.ds(lax.rem(my_x + t, GROUPS) * PEERS, PEERS)]
        pltpu.make_async_copy(mine, mine, ret_val_recv.at[t]).wait()
    owner_col = (iota((PTS, RVES), 1) == target_col).astype(f32)
    vals = dot(owner_col, back_val[:, 0, :])
    vals = jnp.where(iota((PTS, PTS), 1) // 32 == rank_col, vals, 0.0)
    fold = (iota((32, PTS), 1) % 32 == iota((32, PTS), 0)).astype(f32)
    point = dot_t(fold, vals)
    for c in range(3):
        tan_out[c] = point[8 * c + 8:8 * c + 11]

    nodal = gw_ref[0] * point[0:1] + gw_ref[1] * point[1:2] + gw_ref[2] * point[2:3]
    conn = conn_ref[...]
    node_rows = iota((PTS, PTS), 0)
    spread = jnp.zeros((PTS, PTS), f32)
    for a in range(8):
        spread = spread + jnp.where(conn[a:a + 1] == node_rows, nodal[a:a + 1], 0.0)
    local = dot_t(jnp.ones((8, PTS), f32), spread)
    order = order_ref[...]
    order_hot = (iota((PTS, PTS), 0) == order).astype(f32)
    grid = dot(local, order_hot)[0:1]
    halo_src[...] = grid
    turns = [(ds, dr) for ds in (-1, 0, 1) for dr in (-1, 0, 1) if (ds, dr) != (0, 0)]
    copies = []
    for i, (ds, dr) in enumerate(turns):
        to_slab = (below, slab, above)[ds + 1]
        to_rve = (left, me, right)[dr + 1]
        copies.append(pltpu.make_async_remote_copy(
            src_ref=halo_src, dst_ref=halo_dst.at[i], send_sem=halo_send.at[i], recv_sem=halo_recv.at[i],
            device_id=(to_slab, to_rve), device_id_type=MESH))
        copies[i].start()

    for t in range(GROUPS):
        mine = back_phi.at[pl.ds(lax.rem(my_x + t, GROUPS) * PEERS, PEERS)]
        pltpu.make_async_copy(mine, mine, ret_phi_recv.at[t]).wait()
    slot_cols = iota((PTS, RVES * 8), 1)
    hot = jnp.concatenate([(slot_cols == place_col).astype(f32), (slot_cols == place_col + 4).astype(f32)], axis=0)
    found = pick(hot, back_phi[...].reshape(RVES * 8, HALF))
    pot_out[:, :HALF] = found[:PTS]
    pot_out[:, HALF:] = found[PTS:]

    lane = iota((1, PTS), 1)
    at_i, at_j = lane // 15, lane // 5 % 3
    total = grid
    for i, (ds, dr) in enumerate(turns):
        copies[i].wait_recv()
        ok = lane < NODES
        if dr != 0:
            ok = ok & (at_i == (0 if dr > 0 else 2)) & ((me > 0) if dr > 0 else (me < RVES - 1))
        if ds != 0:
            ok = ok & (at_j == (0 if ds > 0 else 2)) & ((slab > 0) if ds > 0 else (slab < SLABS - 1))
        shift = (-30 * dr - 10 * ds) % PTS
        moved = pltpu.roll(jnp.broadcast_to(halo_dst[i], (8, PTS)), shift, 1)[0:1]
        total = total + jnp.where(ok, moved, 0.0)
    total = jnp.where(lane < NODES, total, 0.0)
    back = dot_t(jnp.broadcast_to(total, (8, PTS)), order_hot)
    res_out[...] = back[0:1, :NODES]

    for copy in copies:
        copy.wait_send()
    for t in range(GROUPS):
        n = PEERS - 1 if t == 0 else PEERS
        pltpu.make_async_copy(send_phi.at[pl.ds(0, n)], send_phi.at[pl.ds(0, n)], out_phi_send.at[t]).wait()
        pltpu.make_async_copy(send_mac.at[pl.ds(0, n)], send_mac.at[pl.ds(0, n)], out_mac_send.at[t]).wait()
        pltpu.make_async_copy(send_phi.at[pl.ds(0, n)], send_phi.at[pl.ds(0, n)], ret_phi_send.at[t]).wait()
        pltpu.make_async_copy(send_mac.at[pl.ds(0, n)], send_mac.at[pl.ds(0, n)], ret_val_send.at[t]).wait()


def on_device(
    macro_field, rve_owner, potential, switch_words, permeability, coercivity, grain_axes,
    hyst_axis, hyst_low, hyst_high, hyst_weight, grad_weights, connectivity, node_order,
):
    vmem = pl.BlockSpec(memory_space=pltpu.VMEM)
    smem = pl.BlockSpec(memory_space=pltpu.SMEM)
    hbm = pl.BlockSpec(memory_space=pl.ANY)
    order = jnp.pad(node_order, (0, PTS - NODES), constant_values=-1).reshape(1, PTS)
    pot, tan, res = pl.pallas_call(
        kernel,
        out_shape=(
            jax.ShapeDtypeStruct((PTS, 2 * HALF), f32),
            jax.ShapeDtypeStruct((3, 3, PTS), f32),
            jax.ShapeDtypeStruct((1, NODES), f32),
        ),
        in_specs=[vmem, vmem, vmem, hbm, hbm, hbm, hbm, smem, smem, smem, smem, vmem, vmem, vmem],
        out_specs=(vmem, vmem, vmem),
        scratch_shapes=[
            pltpu.VMEM((GROUPS, SLOTS, 2 * HALF), jnp.int32),
            pltpu.VMEM((GROUPS, SLOTS, 2 * HALF), f32),
            pltpu.VMEM((GROUPS, SLOTS, 2 * HALF), f32),
            pltpu.VMEM((GROUPS, 3, SLOTS, 2 * HALF), f32),
            pltpu.VMEM((4, 8, 8, PTS), jnp.int32),
            pltpu.VMEM((N_FIELDS, 4, 8, 8, PTS), f32),
            pltpu.VMEM((RVES, 8, HALF), f32),
            pltpu.VMEM((RVES, 1, PTS), f32),
            pltpu.VMEM((GROUPS, PEERS, 8, HALF), f32),
            pltpu.VMEM((GROUPS, PEERS, 1, PTS), f32),
            pltpu.VMEM((GROUPS, PEERS // 2, 2, 8, HALF), f32),
            pltpu.VMEM((GROUPS, PEERS, 1, PTS), f32),
            pltpu.VMEM((RVES, 8, HALF), f32),
            pltpu.VMEM((RVES, 1, PTS), f32),
            pltpu.VMEM((96, PTS), f32),
            pltpu.VMEM((1, PTS), f32),
            pltpu.VMEM((8, 1, PTS), f32),
            pltpu.SemaphoreType.DMA((4, GROUPS)),
        ] + [pltpu.SemaphoreType.DMA((GROUPS,))] * 8 + [pltpu.SemaphoreType.DMA((8,))] * 2,
        compiler_params=pltpu.CompilerParams(
            collective_id=0, has_side_effects=True, vmem_limit_bytes=48 * 1024 * 1024),
    )(rve_owner.reshape(1, PTS), macro_field, potential, switch_words, permeability, coercivity, grain_axes,
      hyst_axis, hyst_low, hyst_high, hyst_weight, grad_weights, connectivity, order)
    return pot, tan, res.reshape(NODES)


def solution(mesh):
    return jax.shard_map(
        on_device,
        mesh=mesh,
        in_specs=(
            P(None, ("slab", "rve")),
            P(("slab", "rve"), None),
            P(("slab", "rve"), None),
            P(("slab", "rve"), None),
            P(("slab", "rve"), None),
            P(("slab", "rve"), None),
            P(None, ("slab", "rve"), None),
            P(),
            P(),
            P(),
            P(),
            P(None, None, ("slab", "rve")),
            P(None, ("slab", "rve")),
            P(("slab", "rve")),
        ),
        out_specs=(P(("slab", "rve"), None), P(None, None, ("slab", "rve")), P(("slab", "rve"))),
        check_vma=False,
    )
```

time: 293 us -> 74.9 us (0.26); the launches traced: 288 us -> 74.4 us
  other arithmetic: 87.6 us -> 0 us
  starting transfers between devices: 66 us -> 0 us
  Pallas kernels: 0 us -> 60.5 us
  local copies, waits for them, and re-layouts: 68.1 us -> 13.3 us
  between operations: 50.2 us -> 0.65 us
  waiting for transfers between devices: 12.8 us -> 0 us
  matrix products: 3.33 us -> 0 us
    pallas_call x0 -> x1, Pallas kernels: none -> 60.5 us  [on_device(): pl.pallas_call(kernel, out_shape=(jax.ShapeDtypeStruct((PTS, 2 * HALF), f...]
    all_to_all x5 -> x0, starting transfers between devices: 56.1 us -> none  [the longest x1 14.8 us: on_device(): lax.all_to_all(send_field, 'rve', split_axis=0, concat_axis=0, tiled=True)]
    slice x156 -> x0, local copies, waits for them, and re-layouts: 50.9 us -> none  [the longest x38 19.2 us: neighbour(): within = jnp.roll(values, -stride, axis=-1)]
    add x20 -> x0, other arithmetic: 39.9 us -> none  [the longest x10 30 us: evaluate(): tangent_local[left_comp][0] * gradients[0][column]]
    mul x11 -> x0, other arithmetic: 20.9 us -> none  [the longest x1 6.45 us: make_thresholds(): coerc * jnp.where(jnp.bitwise_and(jnp.right_shift(words, hysteron), 1) ==...]
    reduce_sum x4 -> x0, other arithmetic: 15.9 us -> none  [the longest x2 11.3 us: micro_solve(): jnp.mean(micro_flux[component], axis=-1)]
    unnamed x86 -> x29, local copies, waits for them, and re-layouts: 1.69 us -> 12.7 us
    ppermute x4 -> x0, starting transfers between devices: 9.93 us -> none  [the longest x2 6.74 us: extended(): lax.ppermute(lax.slice_in_dim(block, block.shape[dim] - width, None, axis...]
  transfers between devices with their start and end apart: 9 -> 0, of which waited for: 4 -> 0; matrix products, arithmetic and copies ran while one was open for 12% -> 0% of each run, Pallas kernels for 0% -> 0%
where the time goes in v1:
time: 74.9 us; the launch traced here: 74.4 us
  Pallas kernels  60.5 us (81%)
  local copies, waits for them, and re-layouts  13.3 us (18%)
    pallas_call x1, Pallas kernels, on_device(): pl.pallas_call(kernel, out_shape=(jax.ShapeDtypeStruct((PTS, 2 * HALF), f...  60.5 us
    unnamed x29, local copies, waits for them, and re-layouts  12.7 us

profile of v1, /device:TPU:1, one launch (start us, length us, event | category | flops | bytes accessed | tf_op | source)
XLA Modules:
  0.0 74.4 jit_solution(6358803746461945592)
XLA Ops:
  0.6 0.7 pad_bitcast_fusion.order_ref
  1.3 1.4 %copy-done = f32[3,256,512]{2,1,0:T(8,128)S(1)} copy-done((f32[3,256,512]{2,1,0:T(8,128)S(1)}, f32[3,256,512]{2,1,0:T(8,128)}, u32[]{:S(2)}) %copy-start) | copy-done | bytes 1572888
  2.7 0.0 copy-start.1
  2.7 1.0 %copy-done.1 = s32[256,512]{1,0:T(8,128)S(1)} copy-done((s32[256,512]{1,0:T(8,128)S(1)}, s32[256,512]{1,0:T(8,128)}, u32[]{:S(2)}) %copy-start.1) | copy-done | bytes 524312
  3.7 0.0 copy-start.2
  3.7 1.0 %copy-done.2 = f32[256,512]{1,0:T(8,128)S(1)} copy-done((f32[256,512]{1,0:T(8,128)S(1)}, f32[256,512]{1,0:T(8,128)}, u32[]{:S(2)}) %copy-start.2) | copy-done | bytes 524312
  4.8 0.0 copy-start.3
  4.8 1.0 %copy-done.3 = f32[256,512]{1,0:T(8,128)S(1)} copy-done((f32[256,512]{1,0:T(8,128)S(1)}, f32[256,512]{1,0:T(8,128)}, u32[]{:S(2)}) %copy-start.3) | copy-done | bytes 524312
  5.8 0.0 copy-start.4
  5.8 0.9 %copy-done.4 = f32[128,512]{1,0:T(8,128)S(1)} copy-done((f32[128,512]{1,0:T(8,128)S(1)}, f32[128,512]{1,0:T(8,128)}, u32[]{:S(2)}) %copy-start.4) | copy-done | bytes 262168
  6.8 0.0 copy-start.5
  6.8 0.7 copy-done.5
  7.5 0.0 copy-start.6
  7.5 0.7 copy-done.6
  8.2 0.7 copy-done.7
  8.9 0.7 copy-done.8
  9.5 0.7 copy-done.9
  10.2 0.7 copy-done.10
  10.8 0.7 copy-done.11
  11.5 0.7 copy-done.12
  12.2 60.5 %shard_map.157 = (f32[128,512]{1,0:T(8,128)S(1)}, f32[3,3,128]{2,1,0:T(4,128)S(1)}, f32[1,45]{1,0:T(1,128)S(1)}) custom-call(s32[1,128]{1,0:T(1,128)S(1)} %bitcast.4, f32[3,128]{1,0:T(4,128)S(1)} %copy-done.7, f32[128,512]{1,0:T(8,128)S(1)} %copy-done.4, s32[256,512]{1,0:T(8,128)S(1)} %copy-done.1, f32[256,512]{1,0:T(8,128)S(1)} %copy-done.2, ...), custom_call_target="tpu_custom_call" | custom-call | tf_op jit(solution)/shard_map/pallas_call | solution.py:471
  72.6 0.7 copy.20
  73.3 0.6 copy.21
  73.9 0.5 copy.22
  (7 shorter events, 0.0 us)
Async XLA Ops:
  1.3 1.4 %copy-start = (f32[3,256,512]{2,1,0:T(8,128)S(1)}, f32[3,256,512]{2,1,0:T(8,128)}, u32[]{:S(2)}) copy-start(f32[3,256,512]{2,1,0:T(8,128)} %grain_hbm.1) | copy-start | bytes 4718596
  2.7 1.0 %copy-start.1 = (s32[256,512]{1,0:T(8,128)S(1)}, s32[256,512]{1,0:T(8,128)}, u32[]{:S(2)}) copy-start(s32[256,512]{1,0:T(8,128)} %words_hbm.1) | copy-start | bytes 1572868
  3.7 1.0 %copy-start.2 = (f32[256,512]{1,0:T(8,128)S(1)}, f32[256,512]{1,0:T(8,128)}, u32[]{:S(2)}) copy-start(f32[256,512]{1,0:T(8,128)} %perm_hbm.1) | copy-start | bytes 1572868
  4.8 1.0 %copy-start.3 = (f32[256,512]{1,0:T(8,128)S(1)}, f32[256,512]{1,0:T(8,128)}, u32[]{:S(2)}) copy-start(f32[256,512]{1,0:T(8,128)} %coer_hbm.1) | copy-start | bytes 1572868
  5.8 0.9 %copy-start.4 = (f32[128,512]{1,0:T(8,128)S(1)}, f32[128,512]{1,0:T(8,128)}, u32[]{:S(2)}) copy-start(f32[128,512]{1,0:T(8,128)} %pot_ref.1) | copy-start | bytes 786436
  6.8 0.7 copy-start.5
  7.5 0.7 copy-start.6
  8.2 0.7 copy-start.7
  8.9 0.7 copy-start.8
  9.5 0.7 copy-start.9
  10.2 0.7 copy-start.10
  10.8 0.7 copy-start.11
  11.5 0.7 copy-start.12

commit v2 on v1

--- a/solution.py
+++ b/solution.py
@@ -18,6 +18,8 @@
 PTS = 128
 HALF = 256
 NODES = 45
+ROWS = 48
+UNROLL = (7, 7, 8, 8)
 
 PERM = 0
 GRAIN = 1
@@ -35,23 +37,25 @@
     return lax.broadcasted_iota(jnp.int32, shape, dim)
 
 
-def dot(a, b):
-    return lax.dot_general(a, b, (((1,), (0,)), ((), ())), precision=lax.Precision.HIGHEST,
-                           preferred_element_type=f32)
-
-
-def dot_t(a, b):
-    return lax.dot_general(a, b, (((1,), (1,)), ((), ())), precision=lax.Precision.HIGHEST,
-                           preferred_element_type=f32)
-
-
-def pick(hot, data):
+def parts(data):
+    high = data.astype(bf16)
+    return high, (data - high.astype(f32)).astype(bf16)
+
+
+def mm(a, b, dim):
+    return lax.dot_general(a, b, (((1,), (dim,)), ((), ())), preferred_element_type=f32)
+
+
+def dot(hot, data):
+    high, low = parts(data)
     hot = hot.astype(bf16)
-    high = data.astype(bf16)
-    low = (data - high.astype(f32)).astype(bf16)
-    one = lax.dot_general(hot, high, (((1,), (0,)), ((), ())), preferred_element_type=f32)
-    two = lax.dot_general(hot, low, (((1,), (0,)), ((), ())), preferred_element_type=f32)
-    return one + two
+    return mm(hot, high, 0) + mm(hot, low, 0)
+
+
+def dot_t(hot, data):
+    high, low = parts(data)
+    hot = hot.astype(bf16)
+    return mm(hot, high, 1) + mm(hot, low, 1)
 
 
 def swap(v):
@@ -94,9 +98,10 @@
 
 
 def kernel(
-    owner_ref, macro_ref, pot_ref, words_hbm, perm_hbm, coer_hbm, grain_hbm,
-    axis_ref, low_ref, high_ref, weight_ref, gw_ref, conn_ref, order_ref,
+    owner_hbm, macro_hbm, pot_hbm, words_hbm, perm_hbm, coer_hbm, grain_hbm,
+    axis_hbm, low_hbm, high_hbm, weight_hbm, gw_hbm, conn_hbm, order_hbm,
     pot_out, tan_out, res_out,
+    owner_ref, macro_ref, pot_ref, axis_ref, low_ref, high_ref, weight_ref, gw_ref, conn_ref, order_ref, early_sem,
     nat_words, nat_perm, nat_coer, nat_grain, words_t, fields,
     send_phi, send_mac, recv_phi, recv_mac, ret_phi, ret_val, back_phi, back_val,
     acc_ref, halo_src, halo_dst,
@@ -108,7 +113,6 @@
     my_x = lax.div(me, PEERS)
     my_low = lax.rem(me, PEERS)
     right, left = lax.rem(me + 1, RVES), lax.rem(me + RVES - 1, RVES)
-    above, below = lax.rem(slab + 1, SLABS), lax.rem(slab + SLABS - 1, SLABS)
 
     barrier = pltpu.get_barrier_semaphore()
 
@@ -118,9 +122,29 @@
         return carry
 
     lax.fori_loop(1, RVES, greet, 0)
-    for s in (above, below):
-        for r in (left, me, right):
-            pl.semaphore_signal(barrier, inc=1, device_id=(s, r), device_id_type=MESH)
+
+    def toward(ds, action):
+        if ds == 0:
+            action()
+        else:
+            pl.when((slab > 0) if ds < 0 else (slab < SLABS - 1))(action)
+
+    for ds in (-1, 1):
+        def hail(ds=ds):
+            for r in (left, me, right):
+                pl.semaphore_signal(barrier, inc=1, device_id=(slab + ds, r), device_id_type=MESH)
+
+        toward(ds, hail)
+
+    early = [
+        pltpu.make_async_copy(src, dst, early_sem.at[i])
+        for i, (src, dst) in enumerate((
+            (owner_hbm, owner_ref), (pot_hbm, pot_ref), (macro_hbm, macro_ref), (axis_hbm, axis_ref),
+            (low_hbm, low_ref), (high_hbm, high_ref), (weight_hbm, weight_ref), (gw_hbm, gw_ref),
+            (conn_hbm, conn_ref), (order_hbm, order_ref)))
+    ]
+    for copy in early:
+        copy.start()
 
     def loads(t):
         rows = pl.ds(lax.rem(my_x - t + GROUPS, GROUPS) * SLOTS, SLOTS)
@@ -135,6 +159,7 @@
         for copy in loads(t):
             copy.start()
 
+    early[0].wait()
     target_row = owner_ref[...]
     target_rows = jnp.broadcast_to(target_row.astype(f32), (PTS, PTS))
     target_cols = target_rows.T
@@ -146,10 +171,12 @@
     place_row = target_row * 8 + rank_row
     place_col = target_col * 8 + rank_col
 
+    for copy in early[1:]:
+        copy.wait()
     slot_rows = iota((RVES * 8, PTS), 0)
     hot = jnp.concatenate([(slot_rows == place_row).astype(f32), (slot_rows == place_row + 4).astype(f32)], axis=1)
     halves = jnp.concatenate([pot_ref[:, :HALF], pot_ref[:, HALF:]], axis=0)
-    send_phi[...] = pick(hot, halves).reshape(RVES, 8, HALF)
+    send_phi[...] = dot(hot, halves).reshape(RVES, 8, HALF)
 
     n_rows = iota((PTS, PTS), 0)
     comp = n_rows // CAP
@@ -158,13 +185,19 @@
     owner_hot = (iota((RVES, PTS), 0) == target_row).astype(f32)
     send_mac[...] = dot_t(owner_hot, spread).reshape(RVES, 1, PTS)
 
-    pl.semaphore_wait(barrier, RVES - 1 + 6)
+    sides = lax.div(slab + SLABS - 1, SLABS) + lax.div(2 * SLABS - 2 - slab, SLABS)
+    pl.semaphore_wait(barrier, RVES - 1 + 3 * sides)
+
+    def partner(i):
+        k = lax.div(i, 2)
+        step = lax.div(k + 1, 2) * (2 * lax.rem(k, 2) - 1)
+        return lax.rem(my_low + 2 * step + PEERS + lax.rem(i, 2) * (1 - 2 * lax.rem(my_low, 2)), PEERS)
 
     def send(t):
         peer_x = lax.rem(my_x + t, GROUPS)
 
         def one(i, carry):
-            peer = peer_x * PEERS + lax.rem(my_low + i, PEERS)
+            peer = peer_x * PEERS + partner(i)
 
             @pl.when(peer != me)
             def _():
@@ -188,6 +221,12 @@
 
     for t in range(GROUPS):
         send(t)
+
+    order_row = jnp.sum(jnp.where(iota((PTS, NODES), 0) == iota((PTS, NODES), 1), order_ref[...].astype(f32), 0.0),
+                        axis=1, keepdims=True)
+    order_cols = jnp.where(iota((PTS, PTS), 0) < NODES, jnp.broadcast_to(order_row, (PTS, PTS)), -1.0)
+    order_row = order_cols.T[:1].astype(jnp.int32)
+    order_col = order_cols[:ROWS].astype(jnp.int32)
 
     lane_peer = iota((PTS, PEERS), 0) // CAP % PEERS
     peer_t = (lane_peer == iota((PTS, PEERS), 1)).astype(f32)
@@ -277,7 +316,7 @@
             apply(y, first, sums)
             return nxt
 
-        carry = lax.fori_loop(1, 8, step, carry)
+        carry = lax.fori_loop(1, 8, step, carry, unroll=UNROLL[0 if first else 1])
         apply(0, first, close(force, weight, forces, carry))
 
     def last(mean):
@@ -299,7 +338,7 @@
 
         zero = jnp.zeros((4, 8, PTS), f32)
         flat = jnp.zeros((8, PTS), f32)
-        prev, acc = lax.fori_loop(0, 8, step, ((zero,) * 3, (flat,) * 18))
+        prev, acc = lax.fori_loop(0, 8, step, ((zero,) * 3, (flat,) * 18), unroll=UNROLL[2])
         psi = [fields[PSI + 3 + d, :, 0] for d in range(3)]
         for c in range(3):
             acc_ref[8 * c:8 * c + 8] = acc[c]
@@ -339,7 +378,7 @@
                 fields[AIJ + i, :, y] = pg[a] * grain[b]
             return carry
 
-        lax.fori_loop(0, 8, prepare, 0)
+        lax.fori_loop(0, 8, prepare, 0, unroll=UNROLL[3])
 
         pltpu.make_async_copy(recv_phi.at[t], recv_phi.at[t], out_phi_recv.at[t]).wait()
         pltpu.make_async_copy(recv_mac.at[t], recv_mac.at[t], out_mac_recv.at[t]).wait()
@@ -365,7 +404,7 @@
 
         def give(src, dst, send_sem, recv_sem):
             def one(i, carry):
-                low = lax.rem(my_low + i, PEERS)
+                low = partner(i)
                 peer = src_x * PEERS + low
                 piece = src(low)
 
@@ -383,11 +422,15 @@
 
             lax.fori_loop(0, PEERS, one, 0)
 
-        give(lambda low: ret_phi.at[t, lax.div(low, 2), lax.rem(low, 2)], back_phi, ret_phi_send, ret_phi_recv)
+        def give_phi():
+            give(lambda low: ret_phi.at[t, lax.div(low, 2), lax.rem(low, 2)], back_phi, ret_phi_send, ret_phi_recv)
+
+        pl.when(t < GROUPS - 1)(give_phi)
         last(mean)
         val = jnp.where(mask_val, dot(val_hot, acc_ref[...]), 0.0)
         ret_val[t] = dot_t(peer_m, val).reshape(PEERS, 1, PTS)
         give(lambda low: ret_val.at[t, low], back_val, ret_val_send, ret_val_recv)
+        pl.when(t == GROUPS - 1)(give_phi)
         return carry
 
     lax.fori_loop(0, GROUPS, group, 0)
@@ -405,31 +448,29 @@
 
     nodal = gw_ref[0] * point[0:1] + gw_ref[1] * point[1:2] + gw_ref[2] * point[2:3]
     conn = conn_ref[...]
-    node_rows = iota((PTS, PTS), 0)
-    spread = jnp.zeros((PTS, PTS), f32)
+    spread = jnp.zeros((ROWS, PTS), f32)
     for a in range(8):
-        spread = spread + jnp.where(conn[a:a + 1] == node_rows, nodal[a:a + 1], 0.0)
-    local = dot_t(jnp.ones((8, PTS), f32), spread)
-    order = order_ref[...]
-    order_hot = (iota((PTS, PTS), 0) == order).astype(f32)
-    grid = dot(local, order_hot)[0:1]
+        spread = spread + jnp.where(conn[a:a + 1] == order_col, nodal[a:a + 1], 0.0)
+    spread = jnp.concatenate([spread, jnp.zeros((PTS - ROWS, PTS), f32)], axis=0)
+    grid = dot_t(jnp.ones((8, PTS), f32), spread)[0:1]
     halo_src[...] = grid
     turns = [(ds, dr) for ds in (-1, 0, 1) for dr in (-1, 0, 1) if (ds, dr) != (0, 0)]
-    copies = []
-    for i, (ds, dr) in enumerate(turns):
-        to_slab = (below, slab, above)[ds + 1]
-        to_rve = (left, me, right)[dr + 1]
-        copies.append(pltpu.make_async_remote_copy(
+    copies = [
+        pltpu.make_async_remote_copy(
             src_ref=halo_src, dst_ref=halo_dst.at[i], send_sem=halo_send.at[i], recv_sem=halo_recv.at[i],
-            device_id=(to_slab, to_rve), device_id_type=MESH))
-        copies[i].start()
-
+            device_id=(slab + ds, (left, me, right)[dr + 1]), device_id_type=MESH)
+        for i, (ds, dr) in enumerate(turns)]
+    for (ds, dr), copy in zip(turns, copies):
+        toward(ds, copy.start)
+
+    found = jnp.zeros((2 * PTS, HALF), f32)
     for t in range(GROUPS):
-        mine = back_phi.at[pl.ds(lax.rem(my_x + t, GROUPS) * PEERS, PEERS)]
+        base = lax.rem(my_x + t, GROUPS) * PEERS
+        mine = back_phi.at[pl.ds(base, PEERS)]
         pltpu.make_async_copy(mine, mine, ret_phi_recv.at[t]).wait()
-    slot_cols = iota((PTS, RVES * 8), 1)
-    hot = jnp.concatenate([(slot_cols == place_col).astype(f32), (slot_cols == place_col + 4).astype(f32)], axis=0)
-    found = pick(hot, back_phi[...].reshape(RVES * 8, HALF))
+        slot_cols = iota((PTS, PEERS * 8), 1) + base * 8
+        hot = jnp.concatenate([(slot_cols == place_col).astype(f32), (slot_cols == place_col + 4).astype(f32)], axis=0)
+        found = found + dot(hot, mine[...].reshape(PEERS * 8, HALF))
     pot_out[:, :HALF] = found[:PTS]
     pot_out[:, HALF:] = found[PTS:]
 
@@ -437,7 +478,7 @@
     at_i, at_j = lane // 15, lane // 5 % 3
     total = grid
     for i, (ds, dr) in enumerate(turns):
-        copies[i].wait_recv()
+        toward(-ds, copies[i].wait_recv)
         ok = lane < NODES
         if dr != 0:
             ok = ok & (at_i == (0 if dr > 0 else 2)) & ((me > 0) if dr > 0 else (me < RVES - 1))
@@ -447,11 +488,13 @@
         moved = pltpu.roll(jnp.broadcast_to(halo_dst[i], (8, PTS)), shift, 1)[0:1]
         total = total + jnp.where(ok, moved, 0.0)
     total = jnp.where(lane < NODES, total, 0.0)
-    back = dot_t(jnp.broadcast_to(total, (8, PTS)), order_hot)
+    high, low = parts(jnp.broadcast_to(total, (8, PTS)))
+    node_hot = (iota((ROWS, PTS), 0) == order_row).astype(bf16)
+    back = mm(high, node_hot, 1) + mm(low, node_hot, 1)
     res_out[...] = back[0:1, :NODES]
 
-    for copy in copies:
-        copy.wait_send()
+    for (ds, dr), copy in zip(turns, copies):
+        toward(ds, copy.wait_send)
     for t in range(GROUPS):
         n = PEERS - 1 if t == 0 else PEERS
         pltpu.make_async_copy(send_phi.at[pl.ds(0, n)], send_phi.at[pl.ds(0, n)], out_phi_send.at[t]).wait()
@@ -465,19 +508,28 @@
     hyst_axis, hyst_low, hyst_high, hyst_weight, grad_weights, connectivity, node_order,
 ):
     vmem = pl.BlockSpec(memory_space=pltpu.VMEM)
-    smem = pl.BlockSpec(memory_space=pltpu.SMEM)
-    hbm = pl.BlockSpec(memory_space=pl.ANY)
-    order = jnp.pad(node_order, (0, PTS - NODES), constant_values=-1).reshape(1, PTS)
+    hbm = pl.BlockSpec(memory_space=pltpu.HBM)
     pot, tan, res = pl.pallas_call(
         kernel,
         out_shape=(
-            jax.ShapeDtypeStruct((PTS, 2 * HALF), f32),
-            jax.ShapeDtypeStruct((3, 3, PTS), f32),
-            jax.ShapeDtypeStruct((1, NODES), f32),
+            pltpu.VMEM((PTS, 2 * HALF), f32),
+            pltpu.VMEM((3, 3, PTS), f32),
+            pltpu.VMEM((1, NODES), f32),
         ),
-        in_specs=[vmem, vmem, vmem, hbm, hbm, hbm, hbm, smem, smem, smem, smem, vmem, vmem, vmem],
+        in_specs=[hbm] * 14,
         out_specs=(vmem, vmem, vmem),
         scratch_shapes=[
+            pltpu.VMEM((1, PTS), jnp.int32),
+            pltpu.VMEM((3, PTS), f32),
+            pltpu.VMEM((PTS, 2 * HALF), f32),
+            pltpu.SMEM((3, 4), f32),
+            pltpu.SMEM((4,), f32),
+            pltpu.SMEM((4,), f32),
+            pltpu.SMEM((4,), f32),
+            pltpu.VMEM((3, 8, PTS), f32),
+            pltpu.VMEM((8, PTS), jnp.int32),
+            pltpu.VMEM((1, NODES), jnp.int32),
+            pltpu.SemaphoreType.DMA((10,)),
             pltpu.VMEM((GROUPS, SLOTS, 2 * HALF), jnp.int32),
             pltpu.VMEM((GROUPS, SLOTS, 2 * HALF), f32),
             pltpu.VMEM((GROUPS, SLOTS, 2 * HALF), f32),
@@ -498,9 +550,9 @@
             pltpu.SemaphoreType.DMA((4, GROUPS)),
         ] + [pltpu.SemaphoreType.DMA((GROUPS,))] * 8 + [pltpu.SemaphoreType.DMA((8,))] * 2,
         compiler_params=pltpu.CompilerParams(
-            collective_id=0, has_side_effects=True, vmem_limit_bytes=48 * 1024 * 1024),
+            collective_id=0, has_side_effects=True, vmem_limit_bytes=60 * 1024 * 1024),
     )(rve_owner.reshape(1, PTS), macro_field, potential, switch_words, permeability, coercivity, grain_axes,
-      hyst_axis, hyst_low, hyst_high, hyst_weight, grad_weights, connectivity, order)
+      hyst_axis, hyst_low, hyst_high, hyst_weight, grad_weights, connectivity, node_order.reshape(1, NODES))
     return pot, tan, res.reshape(NODES)
 
 

time: 74.9 us -> 52.6 us (0.70)
  local copies, waits for them, and re-layouts: 13.3 us -> 1.81 us
  Pallas kernels: 60.5 us -> 49.3 us
    pallas_call x1, Pallas kernels: 60.5 us -> 49.3 us  [on_device(): pl.pallas_call(kernel, out_shape=(pltpu.VMEM((PTS, 2 * HALF), f32), pltpu...]
    unnamed x29 -> x3, local copies, waits for them, and re-layouts: 12.7 us -> 1.81 us
where the time goes in v2:
time: 52.6 us; the launch traced here: 51.7 us
  Pallas kernels  49.3 us (94%)
  local copies, waits for them, and re-layouts  1.81 us (3%)
  between operations  0.65 us (1%)
    pallas_call x1, Pallas kernels, on_device(): pl.pallas_call(kernel, out_shape=(pltpu.VMEM((PTS, 2 * HALF), f32), pltpu...  49.3 us
    unnamed x3, local copies, waits for them, and re-layouts  1.81 us

profile of v2, /device:TPU:1, one launch (start us, length us, event | category | flops | bytes accessed | tf_op | source)
XLA Modules:
  0.0 51.7 jit_solution(16955178084801630897)
XLA Ops:
  0.6 49.3 %shard_map.157 = (f32[128,512]{1,0:T(8,128)S(1)}, f32[3,3,128]{2,1,0:T(4,128)S(1)}, f32[1,45]{1,0:T(1,128)S(1)}) custom-call(s32[1,128]{1,0:T(1,128)} %bitcast.4, f32[3,128]{1,0:T(4,128)} %macro_hbm.1, f32[128,512]{1,0:T(8,128)} %pot_hbm.1, s32[256,512]{1,0:T(8,128)} %words_hbm.1, f32[256,512]{1,0:T(8,128)} %perm_hbm.1, f32[256,512]{1,0:T(8,128)} %coer_hbm.1, ...), custom_call_target="tpu_custom_call" | custom-call | tf_op jit(solution)/shard_map/pallas_call | solution.py:512
  49.9 0.7 %copy.20 = f32[128,512]{1,0:T(8,128)} copy(f32[128,512]{1,0:T(8,128)S(1)} %get-tuple-element.9) | data formatting | bytes 524288
  50.6 0.5 copy.22
  51.2 0.6 %copy.21 = f32[3,3,128]{2,1,0:T(4,128)} copy(f32[3,3,128]{2,1,0:T(4,128)S(1)} %get-tuple-element.10) | data formatting | bytes 9216

commit v3 on v2

--- a/solution.py
+++ b/solution.py
@@ -20,16 +20,17 @@
 NODES = 45
 ROWS = 48
 UNROLL = (7, 7, 8, 8)
+HOLD = 1
 
 PERM = 0
 GRAIN = 1
 TH = 4
 PG = 8
 AIJ = 11
-PHI = 17
-PSI = 20
-COER = 26
-N_FIELDS = 27
+N_HELD = 17
+PHI = 0
+PSI = 3
+N_FIELDS = 9
 PAIRS = ((0, 0), (0, 1), (0, 2), (1, 1), (1, 2), (2, 2))
 
 
@@ -102,9 +103,9 @@
     axis_hbm, low_hbm, high_hbm, weight_hbm, gw_hbm, conn_hbm, order_hbm,
     pot_out, tan_out, res_out,
     owner_ref, macro_ref, pot_ref, axis_ref, low_ref, high_ref, weight_ref, gw_ref, conn_ref, order_ref, early_sem,
-    nat_words, nat_perm, nat_coer, nat_grain, words_t, fields,
+    nat_words, nat_perm, nat_coer, nat_grain, words_t, coer_t, held, fields,
     send_phi, send_mac, recv_phi, recv_mac, ret_phi, ret_val, back_phi, back_val,
-    acc_ref, halo_src, halo_dst,
+    acc_ref, means, halo_src, halo_dst,
     load_sem, out_phi_send, out_phi_recv, out_mac_send, out_mac_recv,
     ret_phi_send, ret_phi_recv, ret_val_send, ret_val_recv, halo_send, halo_recv,
 ):
@@ -114,28 +115,6 @@
     my_low = lax.rem(me, PEERS)
     right, left = lax.rem(me + 1, RVES), lax.rem(me + RVES - 1, RVES)
 
-    barrier = pltpu.get_barrier_semaphore()
-
-    def greet(i, carry):
-        peer = lax.rem(me + i, RVES)
-        pl.semaphore_signal(barrier, inc=1, device_id=(slab, peer), device_id_type=MESH)
-        return carry
-
-    lax.fori_loop(1, RVES, greet, 0)
-
-    def toward(ds, action):
-        if ds == 0:
-            action()
-        else:
-            pl.when((slab > 0) if ds < 0 else (slab < SLABS - 1))(action)
-
-    for ds in (-1, 1):
-        def hail(ds=ds):
-            for r in (left, me, right):
-                pl.semaphore_signal(barrier, inc=1, device_id=(slab + ds, r), device_id_type=MESH)
-
-        toward(ds, hail)
-
     early = [
         pltpu.make_async_copy(src, dst, early_sem.at[i])
         for i, (src, dst) in enumerate((
@@ -143,8 +122,30 @@
             (low_hbm, low_ref), (high_hbm, high_ref), (weight_hbm, weight_ref), (gw_hbm, gw_ref),
             (conn_hbm, conn_ref), (order_hbm, order_ref)))
     ]
-    for copy in early:
+    for copy in early[:3]:
         copy.start()
+
+    barrier = pltpu.get_barrier_semaphore()
+
+    def greet(i, carry):
+        peer = lax.rem(me + i, RVES)
+        pl.semaphore_signal(barrier, inc=1, device_id=(slab, peer), device_id_type=MESH)
+        return carry
+
+    lax.fori_loop(1, RVES, greet, 0, unroll=7)
+
+    def toward(ds, action):
+        if ds == 0:
+            action()
+        else:
+            pl.when((slab > 0) if ds < 0 else (slab < SLABS - 1))(action)
+
+    for ds in (-1, 1):
+        def hail(ds=ds):
+            for r in (left, me, right):
+                pl.semaphore_signal(barrier, inc=1, device_id=(slab + ds, r), device_id_type=MESH)
+
+        toward(ds, hail)
 
     def loads(t):
         rows = pl.ds(lax.rem(my_x - t + GROUPS, GROUPS) * SLOTS, SLOTS)
@@ -155,6 +156,8 @@
             pltpu.make_async_copy(grain_hbm.at[:, rows], nat_grain.at[t], load_sem.at[3, t]),
         )
 
+    for copy in early[3:]:
+        copy.start()
     for t in range(GROUPS):
         for copy in loads(t):
             copy.start()
@@ -171,12 +174,9 @@
     place_row = target_row * 8 + rank_row
     place_col = target_col * 8 + rank_col
 
-    for copy in early[1:]:
-        copy.wait()
-    slot_rows = iota((RVES * 8, PTS), 0)
-    hot = jnp.concatenate([(slot_rows == place_row).astype(f32), (slot_rows == place_row + 4).astype(f32)], axis=1)
-    halves = jnp.concatenate([pot_ref[:, :HALF], pot_ref[:, HALF:]], axis=0)
-    send_phi[...] = dot(hot, halves).reshape(RVES, 8, HALF)
+    early[1].wait()
+    early[2].wait()
+    halves = parts(jnp.concatenate([pot_ref[:, :HALF], pot_ref[:, HALF:]], axis=0))
 
     n_rows = iota((PTS, PTS), 0)
     comp = n_rows // CAP
@@ -193,34 +193,58 @@
         step = lax.div(k + 1, 2) * (2 * lax.rem(k, 2) - 1)
         return lax.rem(my_low + 2 * step + PEERS + lax.rem(i, 2) * (1 - 2 * lax.rem(my_low, 2)), PEERS)
 
+    def issue(t, peer_x, start, start_local):
+        def one(i, carry):
+            low = partner(i)
+            start(low, peer_x * PEERS + low)
+            return carry
+
+        if isinstance(t, int):
+            (start_local if t == 0 else start)(my_low, peer_x * PEERS + my_low)
+        else:
+            @pl.when(t == 0)
+            def _():
+                start_local(my_low, me)
+
+            @pl.when(t > 0)
+            def _():
+                start(my_low, peer_x * PEERS + my_low)
+
+        lax.fori_loop(1, PEERS, one, 0, unroll=5)
+
     def send(t):
-        peer_x = lax.rem(my_x + t, GROUPS)
-
-        def one(i, carry):
-            peer = peer_x * PEERS + partner(i)
-
-            @pl.when(peer != me)
-            def _():
-                pltpu.make_async_remote_copy(
-                    src_ref=send_phi.at[peer], dst_ref=recv_phi.at[t, my_low],
-                    send_sem=out_phi_send.at[t], recv_sem=out_phi_recv.at[t],
-                    device_id=(slab, peer), device_id_type=MESH).start()
-                pltpu.make_async_remote_copy(
-                    src_ref=send_mac.at[peer], dst_ref=recv_mac.at[t, my_low],
-                    send_sem=out_mac_send.at[t], recv_sem=out_mac_recv.at[t],
-                    device_id=(slab, peer), device_id_type=MESH).start()
-
-            @pl.when(peer == me)
-            def _():
-                pltpu.make_async_copy(send_phi.at[peer], recv_phi.at[t, my_low], out_phi_recv.at[t]).start()
-                pltpu.make_async_copy(send_mac.at[peer], recv_mac.at[t, my_low], out_mac_recv.at[t]).start()
-
-            return carry
-
-        lax.fori_loop(0, PEERS, one, 0)
-
-    for t in range(GROUPS):
+        issue(
+            t, lax.rem(my_x + t, GROUPS),
+            lambda low, peer: pltpu.make_async_remote_copy(
+                src_ref=send_phi.at[peer], dst_ref=recv_phi.at[t, my_low],
+                send_sem=out_phi_send.at[t], recv_sem=out_phi_recv.at[t],
+                device_id=(slab, peer), device_id_type=MESH).start(),
+            lambda low, peer: pltpu.make_async_copy(
+                send_phi.at[peer], recv_phi.at[t, my_low], out_phi_recv.at[t]).start())
+
+    def send_field(t):
+        issue(
+            t, lax.rem(my_x + t, GROUPS),
+            lambda low, peer: pltpu.make_async_remote_copy(
+                src_ref=send_mac.at[peer], dst_ref=recv_mac.at[t, my_low],
+                send_sem=out_mac_send.at[t], recv_sem=out_mac_recv.at[t],
+                device_id=(slab, peer), device_id_type=MESH).start(),
+            lambda low, peer: pltpu.make_async_copy(
+                send_mac.at[peer], recv_mac.at[t, my_low], out_mac_recv.at[t]).start())
+
+    slot_rows = iota((PEERS * 8, PTS), 0)
+    for t in range(GROUPS):
+        base = lax.rem(my_x + t, GROUPS) * PEERS
+        rows = slot_rows + base * 8
+        hot = jnp.concatenate([(rows == place_row).astype(f32), (rows == place_row + 4).astype(f32)], axis=1)
+        hot = hot.astype(bf16)
+        send_phi[pl.ds(base, PEERS)] = (mm(hot, halves[0], 0) + mm(hot, halves[1], 0)).reshape(PEERS, 8, HALF)
         send(t)
+        if t == 0:
+            for other in range(GROUPS):
+                send_field(other)
+    for copy in early[3:]:
+        copy.wait()
 
     order_row = jnp.sum(jnp.where(iota((PTS, NODES), 0) == iota((PTS, NODES), 1), order_ref[...].astype(f32), 0.0),
                         axis=1, keepdims=True)
@@ -245,34 +269,34 @@
     low2 = [2.0 * low_ref[k] for k in range(4)]
     high2 = [2.0 * high_ref[k] for k in range(4)]
 
-    def evaluate(y, version, mean):
+    def evaluate(t, y, version, mean):
         now = fields[PHI + version, :, y]
         y_next = fields[PHI + version, :, lax.rem(y + 1, 8)]
         h = [mean[0] + (next_x(now) - now), mean[1] + (y_next - now), mean[2] + (next_z(now) - now)]
-        g = [fields[GRAIN + c, :, y] * h[c] for c in range(3)]
+        g = [held[t, GRAIN + c, :, y] * h[c] for c in range(3)]
         s = []
         for k in range(4):
-            arg = axis2[0][k] * g[0] + axis2[1][k] * g[1] + axis2[2][k] * g[2] - fields[TH + k, :, y]
+            arg = axis2[0][k] * g[0] + axis2[1][k] * g[1] + axis2[2][k] * g[2] - held[t, TH + k, :, y]
             s.append(jnp.tanh(arg))
         slope = [1.0 - v * v for v in s]
-        perm = fields[PERM, :, y]
+        perm = held[t, PERM, :, y]
         flux = []
         for c in range(3):
             mag = mag_w[c][0] * s[0] + mag_w[c][1] * s[1] + mag_w[c][2] * s[2] + mag_w[c][3] * s[3]
-            flux.append(perm * h[c] + fields[PG + c, :, y] * mag)
+            flux.append(perm * h[c] + held[t, PG + c, :, y] * mag)
         stiff = {}
         for i, pair in enumerate(PAIRS):
             w = pair_w[i]
             total = w[0] * slope[0] + w[1] * slope[1] + w[2] * slope[2] + w[3] * slope[3]
-            v = fields[AIJ + i, :, y] * total
+            v = held[t, AIJ + i, :, y] * total
             if pair[0] == pair[1]:
                 v = v + perm
             stiff[pair] = v
             stiff[pair[::-1]] = v
         return now, flux, stiff
 
-    def sweep_body(y, first, mean, carry):
-        now, flux, stiff = evaluate(y, 0 if first else 1, mean)
+    def sweep_body(t, y, first, mean, carry):
+        now, flux, stiff = evaluate(t, y, 0 if first else 1, mean)
         if first:
             lin = stiff
         else:
@@ -308,21 +332,21 @@
                 step = fields[PSI + d, :, y] + step
             fields[PSI + (0 if first else 3) + d, :, y] = step
 
-    def sweep(first, mean):
-        carry, (force, weight, forces) = sweep_body(0, first, mean, None)
+    def sweep(t, first, mean):
+        carry, (force, weight, forces) = sweep_body(t, 0, first, mean, None)
 
         def step(y, carry):
-            nxt, sums = sweep_body(y, first, mean, carry)
+            nxt, sums = sweep_body(t, y, first, mean, carry)
             apply(y, first, sums)
             return nxt
 
         carry = lax.fori_loop(1, 8, step, carry, unroll=UNROLL[0 if first else 1])
         apply(0, first, close(force, weight, forces, carry))
 
-    def last(mean):
+    def last(t, mean):
         def step(y, carry):
             prev, acc = carry
-            now, flux, stiff = evaluate(y, 2, mean)
+            now, flux, stiff = evaluate(t, y, 2, mean)
             psi = [fields[PSI + 3 + d, :, y] for d in range(3)]
             acc = list(acc)
             for c in range(3):
@@ -341,56 +365,60 @@
         prev, acc = lax.fori_loop(0, 8, step, ((zero,) * 3, (flat,) * 18), unroll=UNROLL[2])
         psi = [fields[PSI + 3 + d, :, 0] for d in range(3)]
         for c in range(3):
-            acc_ref[8 * c:8 * c + 8] = acc[c]
+            acc_ref[t, 8 * c:8 * c + 8] = acc[c]
             for d in range(3):
                 pair = PAIRS.index((min(c, d), max(c, d)))
                 k = 3 + 3 * c + d
-                acc_ref[8 * k:8 * k + 8] = acc[3 + pair] - acc[9 + 3 * c + d] + sum_x(prev[c] * psi[d])
+                acc_ref[t, 8 * k:8 * k + 8] = acc[3 + pair] - acc[9 + 3 * c + d] + sum_x(prev[c] * psi[d])
 
     def turn(nat, h):
         a = nat[:, h * PTS:(h + 1) * PTS]
         b = nat[:, HALF + h * PTS:HALF + (h + 1) * PTS]
         return jnp.concatenate([a, b], axis=0).T.reshape(2, 8, 8, PTS)
 
-    def group(t, carry):
+    def ahead(t, carry):
         for copy in loads(t):
             copy.wait()
         for h in range(2):
             xs = slice(2 * h, 2 * h + 2)
             words_t[xs] = turn(nat_words[t], h)
-            fields[COER, xs] = turn(nat_coer[t], h)
-            fields[PERM, xs] = turn(nat_perm[t], h)
+            coer_t[xs] = turn(nat_coer[t], h)
+            held[t, PERM, xs] = turn(nat_perm[t], h)
             for c in range(3):
-                fields[GRAIN + c, xs] = turn(nat_grain[t, c], h)
-
-        def prepare(y, carry):
+                held[t, GRAIN + c, xs] = turn(nat_grain[t, c], h)
+
+        def prepare(y, inner):
             words = words_t[:, y]
-            coer = fields[COER, :, y]
+            coer = coer_t[:, y]
             for k in range(4):
                 up = jnp.bitwise_and(words, 1 << k) != 0
-                fields[TH + k, :, y] = coer * jnp.where(up, low2[k], high2[k])
-            perm = fields[PERM, :, y]
-            grain = [fields[GRAIN + c, :, y] for c in range(3)]
+                held[t, TH + k, :, y] = coer * jnp.where(up, low2[k], high2[k])
+            perm = held[t, PERM, :, y]
+            grain = [held[t, GRAIN + c, :, y] for c in range(3)]
             pg = [perm * grain[c] for c in range(3)]
             for c in range(3):
-                fields[PG + c, :, y] = pg[c]
+                held[t, PG + c, :, y] = pg[c]
             for i, (a, b) in enumerate(PAIRS):
-                fields[AIJ + i, :, y] = pg[a] * grain[b]
-            return carry
+                held[t, AIJ + i, :, y] = pg[a] * grain[b]
+            return inner
 
         lax.fori_loop(0, 8, prepare, 0, unroll=UNROLL[3])
-
+        return carry
+
+    lax.fori_loop(0, GROUPS, ahead, 0)
+    for t in range(GROUPS):
+        pltpu.make_async_copy(recv_mac.at[t], recv_mac.at[t], out_mac_recv.at[t]).wait()
+        mac = dot(peer_t, recv_mac[t, :, 0, :])
+        means[t] = dot_t(comp_m, jnp.where(mask_mac, mac, 0.0))
+    def group(t, carry):
         pltpu.make_async_copy(recv_phi.at[t], recv_phi.at[t], out_phi_recv.at[t]).wait()
-        pltpu.make_async_copy(recv_mac.at[t], recv_mac.at[t], out_mac_recv.at[t]).wait()
         rows = to_rows(recv_phi[t])
         for h in range(2):
             fields[PHI, 2 * h:2 * h + 2] = rows[:, h * PTS:(h + 1) * PTS].T.reshape(2, 8, 8, PTS)
-        mac = dot(peer_t, recv_mac[t, :, 0, :])
-        mac = dot_t(comp_m, jnp.where(mask_mac, mac, 0.0))
-        mean = [jnp.broadcast_to(mac[c:c + 1], (8, PTS))[None] for c in range(3)]
-
-        sweep(True, mean)
-        sweep(False, mean)
+        mean = [jnp.broadcast_to(means[t, c:c + 1], (8, PTS))[None] for c in range(3)]
+
+        sweep(t, True, mean)
+        sweep(t, False, mean)
 
         first = iota((8, 8, PTS), 1) < 4
         for h in range(2):
@@ -400,40 +428,32 @@
             ret_phi[t, :, 0, :, cols] = jnp.where(first, low, pltpu.roll(high, 4, 1))
             ret_phi[t, :, 1, :, cols] = jnp.where(first, pltpu.roll(low, 4, 1), high)
 
-        src_x = lax.rem(my_x - t + GROUPS, GROUPS)
-
-        def give(src, dst, send_sem, recv_sem):
-            def one(i, carry):
-                low = partner(i)
-                peer = src_x * PEERS + low
-                piece = src(low)
-
-                @pl.when(peer != me)
-                def _():
-                    pltpu.make_async_remote_copy(
-                        src_ref=piece, dst_ref=dst.at[me], send_sem=send_sem.at[t], recv_sem=recv_sem.at[t],
-                        device_id=(slab, peer), device_id_type=MESH).start()
-
-                @pl.when(peer == me)
-                def _():
-                    pltpu.make_async_copy(piece, dst.at[me], recv_sem.at[t]).start()
-
-                return carry
-
-            lax.fori_loop(0, PEERS, one, 0)
-
-        def give_phi():
-            give(lambda low: ret_phi.at[t, lax.div(low, 2), lax.rem(low, 2)], back_phi, ret_phi_send, ret_phi_recv)
-
-        pl.when(t < GROUPS - 1)(give_phi)
-        last(mean)
-        val = jnp.where(mask_val, dot(val_hot, acc_ref[...]), 0.0)
+        @pl.when(t < GROUPS - HOLD)
+        def _():
+            give_phi(t)
+
+        last(t, mean)
+        return carry
+
+    def give(t, src, dst, send_sem, recv_sem):
+        issue(
+            t, lax.rem(my_x - t + GROUPS, GROUPS),
+            lambda low, peer: pltpu.make_async_remote_copy(
+                src_ref=src(low), dst_ref=dst.at[me], send_sem=send_sem.at[t], recv_sem=recv_sem.at[t],
+                device_id=(slab, peer), device_id_type=MESH).start(),
+            lambda low, peer: pltpu.make_async_copy(src(low), dst.at[me], recv_sem.at[t]).start())
+
+    def give_phi(t):
+        give(t, lambda low: ret_phi.at[t, lax.div(low, 2), lax.rem(low, 2)], back_phi, ret_phi_send, ret_phi_recv)
+
+    lax.fori_loop(0, GROUPS, group, 0)
+    for t in range(GROUPS):
+        val = jnp.where(mask_val, dot(val_hot, acc_ref[t]), 0.0)
         ret_val[t] = dot_t(peer_m, val).reshape(PEERS, 1, PTS)
-        give(lambda low: ret_val.at[t, low], back_val, ret_val_send, ret_val_recv)
-        pl.when(t == GROUPS - 1)(give_phi)
-        return carry
-
-    lax.fori_loop(0, GROUPS, group, 0)
+    for t in range(GROUPS):
+        give(t, lambda low, t=t: ret_val.at[t, low], back_val, ret_val_send, ret_val_recv)
+    for t in range(GROUPS - HOLD, GROUPS):
+        give_phi(t)
 
     for t in range(GROUPS):
         mine = back_val.at[pl.ds(lax.rem(my_x + t, GROUPS) * PEERS, PEERS)]
@@ -535,6 +555,8 @@
             pltpu.VMEM((GROUPS, SLOTS, 2 * HALF), f32),
             pltpu.VMEM((GROUPS, 3, SLOTS, 2 * HALF), f32),
             pltpu.VMEM((4, 8, 8, PTS), jnp.int32),
+            pltpu.VMEM((4, 8, 8, PTS), f32),
+            pltpu.VMEM((GROUPS, N_HELD, 4, 8, 8, PTS), f32),
             pltpu.VMEM((N_FIELDS, 4, 8, 8, PTS), f32),
             pltpu.VMEM((RVES, 8, HALF), f32),
             pltpu.VMEM((RVES, 1, PTS), f32),
@@ -544,7 +566,8 @@
             pltpu.VMEM((GROUPS, PEERS, 1, PTS), f32),
             pltpu.VMEM((RVES, 8, HALF), f32),
             pltpu.VMEM((RVES, 1, PTS), f32),
-            pltpu.VMEM((96, PTS), f32),
+            pltpu.VMEM((GROUPS, 96, PTS), f32),
+            pltpu.VMEM((GROUPS, 8, PTS), f32),
             pltpu.VMEM((1, PTS), f32),
             pltpu.VMEM((8, 1, PTS), f32),
             pltpu.SemaphoreType.DMA((4, GROUPS)),

time: 52.6 us -> 51 us (0.970)
  Pallas kernels: 49.3 us -> 48 us
    pallas_call x1, Pallas kernels: 49.3 us -> 48 us  [on_device(): pl.pallas_call(kernel, out_shape=(pltpu.VMEM((PTS, 2 * HALF), f32), pltpu...]
where the time goes in v3:
time: 51 us; the launch traced here: 50.5 us
  Pallas kernels  48 us (94%)
  local copies, waits for them, and re-layouts  1.81 us (4%)
  between operations  0.65 us (1%)
    pallas_call x1, Pallas kernels, on_device(): pl.pallas_call(kernel, out_shape=(pltpu.VMEM((PTS, 2 * HALF), f32), pltpu...  48 us
    unnamed x3, local copies, waits for them, and re-layouts  1.81 us

profile of v3, /device:TPU:1, one launch (start us, length us, event | category | flops | bytes accessed | tf_op | source)
XLA Modules:
  0.0 50.5 jit_solution(4818779821852468892)
XLA Ops:
  0.6 48.0 %shard_map.157 = (f32[128,512]{1,0:T(8,128)S(1)}, f32[3,3,128]{2,1,0:T(4,128)S(1)}, f32[1,45]{1,0:T(1,128)S(1)}) custom-call(s32[1,128]{1,0:T(1,128)} %bitcast.4, f32[3,128]{1,0:T(4,128)} %macro_hbm.1, f32[128,512]{1,0:T(8,128)} %pot_hbm.1, s32[256,512]{1,0:T(8,128)} %words_hbm.1, f32[256,512]{1,0:T(8,128)} %perm_hbm.1, f32[256,512]{1,0:T(8,128)} %coer_hbm.1, ...), custom_call_target="tpu_custom_call" | custom-call | tf_op jit(solution)/shard_map/pallas_call | solution.py:532
  48.7 0.7 %copy.20 = f32[128,512]{1,0:T(8,128)} copy(f32[128,512]{1,0:T(8,128)S(1)} %get-tuple-element.9) | data formatting | bytes 524288
  49.4 0.5 %copy.22 = f32[45]{0:T(128)} copy(f32[45]{0:T(128)S(1)} %bitcast.3) | data formatting | bytes 360
  49.9 0.6 %copy.21 = f32[3,3,128]{2,1,0:T(4,128)} copy(f32[3,3,128]{2,1,0:T(4,128)S(1)} %get-tuple-element.10) | data formatting | bytes 9216

commit v4 on v3

--- a/solution.py
+++ b/solution.py
@@ -158,9 +158,6 @@
 
     for copy in early[3:]:
         copy.start()
-    for t in range(GROUPS):
-        for copy in loads(t):
-            copy.start()
 
     early[0].wait()
     target_row = owner_ref[...]
@@ -169,21 +166,10 @@
     same = target_rows == target_cols
     q_row, q_col = iota((PTS, PTS), 1), iota((PTS, PTS), 0)
     rank_row = jnp.sum(jnp.where(same & (q_col < q_row), 1.0, 0.0), axis=0, keepdims=True).astype(jnp.int32)
-    rank_col = jnp.sum(jnp.where(same & (q_row < q_col), 1.0, 0.0), axis=1, keepdims=True).astype(jnp.int32)
-    target_col = target_cols[:, :1].astype(jnp.int32)
     place_row = target_row * 8 + rank_row
-    place_col = target_col * 8 + rank_col
 
     early[1].wait()
-    early[2].wait()
     halves = parts(jnp.concatenate([pot_ref[:, :HALF], pot_ref[:, HALF:]], axis=0))
-
-    n_rows = iota((PTS, PTS), 0)
-    comp = n_rows // CAP
-    spread = jnp.where(comp == 0, macro_ref[0:1], jnp.where(comp == 1, macro_ref[1:2], macro_ref[2:3]))
-    spread = jnp.where((comp < 3) & (n_rows % CAP == rank_row), spread, 0.0)
-    owner_hot = (iota((RVES, PTS), 0) == target_row).astype(f32)
-    send_mac[...] = dot_t(owner_hot, spread).reshape(RVES, 1, PTS)
 
     sides = lax.div(slab + SLABS - 1, SLABS) + lax.div(2 * SLABS - 2 - slab, SLABS)
     pl.semaphore_wait(barrier, RVES - 1 + 3 * sides)
@@ -241,8 +227,21 @@
         send_phi[pl.ds(base, PEERS)] = (mm(hot, halves[0], 0) + mm(hot, halves[1], 0)).reshape(PEERS, 8, HALF)
         send(t)
         if t == 0:
+            early[2].wait()
+            n_rows = iota((PTS, PTS), 0)
+            comp = n_rows // CAP
+            spread = jnp.where(comp == 0, macro_ref[0:1], jnp.where(comp == 1, macro_ref[1:2], macro_ref[2:3]))
+            spread = jnp.where((comp < 3) & (n_rows % CAP == rank_row), spread, 0.0)
+            owner_hot = (iota((RVES, PTS), 0) == target_row).astype(f32)
+            send_mac[...] = dot_t(owner_hot, spread).reshape(RVES, 1, PTS)
             for other in range(GROUPS):
                 send_field(other)
+            for other in range(GROUPS):
+                for copy in loads(other):
+                    copy.start()
+    rank_col = jnp.sum(jnp.where(same & (q_row < q_col), 1.0, 0.0), axis=1, keepdims=True).astype(jnp.int32)
+    target_col = target_cols[:, :1].astype(jnp.int32)
+    place_col = target_col * 8 + rank_col
     for copy in early[3:]:
         copy.wait()
 

time: 51 us -> 51.1 us (level)
  no operation moved by 1% of the time
where the time goes in v4:
time: 51.1 us; the launch traced here: 50.5 us
  Pallas kernels  48 us (94%)
  local copies, waits for them, and re-layouts  1.81 us (4%)
  between operations  0.65 us (1%)
    pallas_call x1, Pallas kernels, on_device(): pl.pallas_call(kernel, out_shape=(pltpu.VMEM((PTS, 2 * HALF), f32), pltpu...  48 us
    unnamed x3, local copies, waits for them, and re-layouts  1.81 us

profile of v4, /device:TPU:1, one launch (start us, length us, event | category | flops | bytes accessed | tf_op | source)
XLA Modules:
  0.0 50.5 jit_solution(14498508659309259202)
XLA Ops:
  0.6 48.0 %shard_map.157 = (f32[128,512]{1,0:T(8,128)S(1)}, f32[3,3,128]{2,1,0:T(4,128)S(1)}, f32[1,45]{1,0:T(1,128)S(1)}) custom-call(s32[1,128]{1,0:T(1,128)} %bitcast.4, f32[3,128]{1,0:T(4,128)} %macro_hbm.1, f32[128,512]{1,0:T(8,128)} %pot_hbm.1, s32[256,512]{1,0:T(8,128)} %words_hbm.1, f32[256,512]{1,0:T(8,128)} %perm_hbm.1, f32[256,512]{1,0:T(8,128)} %coer_hbm.1, ...), custom_call_target="tpu_custom_call" | custom-call | tf_op jit(solution)/shard_map/pallas_call | solution.py:531
  48.7 0.7 %copy.20 = f32[128,512]{1,0:T(8,128)} copy(f32[128,512]{1,0:T(8,128)S(1)} %get-tuple-element.9) | data formatting | bytes 524288
  49.4 0.5 %copy.22 = f32[45]{0:T(128)} copy(f32[45]{0:T(128)S(1)} %bitcast.3) | data formatting | bytes 360
  49.9 0.6 %copy.21 = f32[3,3,128]{2,1,0:T(4,128)} copy(f32[3,3,128]{2,1,0:T(4,128)S(1)} %get-tuple-element.10) | data formatting | bytes 9216
